TPU v7x, 32 devices: a whole 2x2x4 slice. The times are simulated.
32 devices in a mesh: tasks: 8 (over z, x), group: 4 (over y, core).
Axes of the slice: x: 2, y: 2, z: 4, core: 2. Of those that a mesh axis runs over, the one named last changes fastest.
Arguments:
- support_images: bfloat16 [32, 4, 32, 32, 128], P(('tasks', 'group')), may hold values from -6 to 6
- query_images: bfloat16 [32, 6, 32, 32, 128], P(('tasks', 'group')), may hold values from -6 to 6
- support_target: bfloat16 [32, 4, 8, 8, 128], P(('tasks', 'group')), may hold values from -6 to 6
- query_cotangent: bfloat16 [32, 6, 8, 8, 128], P(('tasks', 'group')), may hold values from -6 to 6
- support_count: int32 [32], P(('tasks', 'group')), may hold values from 1 to 4, as said below
- query_count: int32 [32], P(('tasks', 'group')), may hold values from 1 to 6, as said below
- kernel_one: float32 [3, 3, 128, 128], replicated, may hold values from -0.1875 to 0.1875
- kernel_two: float32 [3, 3, 128, 128], replicated, may hold values from -0.1875 to 0.1875
- gain_one: float32 [128], replicated, may hold values from 0.5 to 1.5
- shift_one: float32 [128], replicated, may hold values from -3 to 3
- gain_two: float32 [128], replicated, may hold values from 0.5 to 1.5
- shift_two: float32 [128], replicated, may hold values from -3 to 3
- outer_one: float32 [128, 128], replicated, as said below
- inner_one: float32 [128, 128], replicated, as said below
- taps_one: float32 [9, 9], replicated, as said below
- outer_two: float32 [128, 128], replicated, as said below
- inner_two: float32 [128, 128], replicated, as said below
- taps_two: float32 [9, 9], replicated, as said below
Outputs:
- query_output: bfloat16 [32, 6, 8, 8, 128], P(('tasks', 'group'))
- support_grad: bfloat16 [32, 4, 32, 32, 128], P(('tasks', 'group'))
- query_grad: bfloat16 [32, 6, 32, 32, 128], P(('tasks', 'group'))
- grad_kernel_one: float32 [3, 3, 128, 128], replicated
- grad_kernel_two: float32 [3, 3, 128, 128], replicated
- grad_gain_one: float32 [128], replicated
- grad_shift_one: float32 [128], replicated
- grad_gain_two: float32 [128], replicated
- grad_shift_two: float32 [128], replicated
- grad_outer_one: float32 [128, 128], replicated
- grad_inner_one: float32 [128, 128], replicated
- grad_taps_one: float32 [9, 9], replicated
- grad_outer_two: float32 [128, 128], replicated
- grad_inner_two: float32 [128, 128], replicated
- grad_taps_two: float32 [9, 9], replicated
Inputs may be any that keep to these rules, and one draw needn't show every extreme that they name: Task t uses its first support_count[t] support slots; some task uses all 4. Task t uses its first query_count[t] query slots; some task uses all 6. `outer_one`: the identity plus independent terms. `inner_one`: the identity plus independent terms. `taps_one`: the identity plus independent terms. `outer_two`: the identity plus independent terms. `inner_two`: the identity plus independent terms. `taps_two`: the identity plus independent terms.
All inputs are finite; a program needn't handle non-finite values.
Results may differ from a plain program's by a relative error of at most 0.015.
Values sent between devices are 32-bit elements; how exact they have to be, the bound alone decides.
No kernel may reach another device: no remote copies, remote signals or barrier semaphores. Data moves between devices by JAX's collectives and lax.ppermute only.
A program may use at most 192 MiB of HBM per device.

v0:
```python
from functools import partial
from types import SimpleNamespace

import jax
import jax.numpy as jnp
from jax import lax
from jax.experimental import pallas as pl
from jax.experimental.pallas import tpu as pltpu
from jax.sharding import PartitionSpec as P

STEP_RATE = 0.01
PENALTY = 1.0
EPSILON = 1e-05
C = 128
F32 = jnp.float32
BF16 = jnp.bfloat16
VMEM_BYTES = 57 << 20
VMEM_SMALL = 24 << 20
MIX_ROWS = 64
AXES = ("tasks", "group")


def shift_down(v):
    place = lax.broadcasted_iota(jnp.int32, v.shape, v.ndim - 2)
    return jnp.where(place == 0, 0.0, pltpu.roll(v, 1, v.ndim - 2))


def shift_up(v):
    place = lax.broadcasted_iota(jnp.int32, v.shape, v.ndim - 2)
    return jnp.where(place == 7, 0.0, pltpu.roll(v, 7, v.ndim - 2))


def put(buf, i, start, tiles, m, blocks, v):
    size = v.shape[0]
    nothing = jnp.zeros((8, C), F32)

    def store(block, value):
        lanes = slice(C * block, C * block + C)
        own = value.reshape(size // 2, 16, C).astype(BF16)
        buf[i, 1 + start : 1 + start + size // 2, :, lanes] = own
        if start == 0:
            buf[i, tiles + 1, :, lanes] = jnp.concatenate([value[1], nothing], 0).astype(BF16)
        if start + size // 2 == tiles:
            buf[i, 0, :, lanes] = jnp.concatenate([nothing, value[size - 2]], 0).astype(BF16)

    store(1 + m, v)
    if m == 0:
        store(blocks + 1, shift_up(v))
    if m == blocks - 1:
        store(0, shift_down(v))


def get(ref, i, start, tiles, m):
    return ref[i, start : start + tiles, :, C * m : C * m + C].reshape(tiles // 2, 2, 2, 8, C)


def set_(ref, i, start, tiles, m, v):
    ref[i, start : start + tiles, :, C * m : C * m + C] = v.reshape(tiles, 16, C)


def total(v):
    return jnp.sum(v.reshape(-1, 8, C), axis=0)


def channel(v):
    return jnp.broadcast_to(jnp.sum(v, axis=0, keepdims=True), (8, C))


def loop(count, body, carry=0):
    return lax.fori_loop(0, count, body, carry)


def write_weights(dst, tap):
    for r in range(3):
        for j in range(4):
            for o in range(2):
                s = j - o
                value = tap(r, s).astype(BF16) if 0 <= s <= 2 else jnp.zeros((C, C), BF16)
                row = C * (4 * r + j)
                dst[row : row + C, C * o : C * o + C] = value


def write_weights_back(dst, tap):
    for r in range(3):
        for j in range(4):
            for o in range(2):
                s = j - o
                value = tap(2 - r, 2 - s).astype(BF16) if 0 <= s <= 2 else jnp.zeros((C, C), BF16)
                col = C * (4 * r + j)
                dst[C * o : C * o + C, col : col + C] = value


NN = (((1,), (0,)), ((), ()))
NT = (((1,), (1,)), ((), ()))
TN = (((0,), (0,)), ((), ()))


def dot(a, b, dims=NN):
    return lax.dot_general(a, b, dims, preferred_element_type=F32)


def rows_one(buf, i, q):
    return jnp.concatenate(
        [buf[i, r : r + 16, :, 256 * q : 256 * q + 512].reshape(256, 512) for r in range(3)], 1
    )


def rows_two(buf, first, number):
    return jnp.concatenate(
        [buf[pl.ds(first, number), r : r + 8].reshape(128 * number, 512) for r in range(3)], 1
    )


def by_two(count, work):
    odd = count % 2 == 1

    @pl.when(odd)
    def _():
        work(count - 1, 1, True)

    @pl.when(jnp.logical_not(odd))
    def _():
        work(0, 2, True)

    def step(p, _):
        work(2 * p, 2, False)
        return 0

    lax.fori_loop(jnp.where(odd, 0, 1), count // 2, step, 0)


def conv_all(count, work):
    def step(p, _):
        work(2 * p, 2)
        return 0

    loop(count // 2, step)

    @pl.when(count % 2 == 1)
    def _():
        work(count - 1, 1)


def conv_one(count, pairs, emit, dims=NN):
    def images(first, number):
        for n in range(number):
            for q in range(2):
                value = None
                for buf, weights in pairs:
                    term = dot(rows_one(buf, first + n, q), weights[...], dims)
                    value = term if value is None else value + term
                emit(first + n, q, value)

    conv_all(count, images)


def conv_two(count, pairs, dst, dims=NN):
    def images(first, number):
        value = None
        for buf, weights in pairs:
            term = dot(rows_two(buf, 2 * first, 2 * number), weights[...], dims)
            value = term if value is None else value + term
        dst[pl.ds(2 * first, 2 * number)] = value.reshape(2 * number, 8, 16, 256)

    conv_all((count + 1) // 2, images)


def kernel_grad_one(count, x, d, acc):
    def images(first, number, fresh):
        places = [(first + n, q) for n in range(number) for q in range(2)]
        grads = jnp.concatenate(
            [d[i, 1:17, :, 128 + 256 * q : 384 + 256 * q].reshape(256, 256) for i, q in places], 0
        )
        for r in range(3):
            ins = jnp.concatenate(
                [x[i, r : r + 16, :, 256 * q : 256 * q + 512].reshape(256, 512) for i, q in places],
                0,
            )
            value = dot(ins, grads, TN)
            acc[r] = value if fresh else acc[r] + value

    by_two(count, images)


def kernel_grad_two(count, pairs, acc):
    def images(first, number, fresh):
        at, size = pl.ds(2 * first, 2 * number), 256 * number
        grads = jnp.concatenate([d[at, 1:9, :, 128:384].reshape(size, 256) for _, d in pairs], 0)
        for r in range(3):
            ins = jnp.concatenate([x[at, r : r + 8].reshape(size, 512) for x, _ in pairs], 0)
            value = dot(ins, grads, TN)
            acc[r] = value if fresh else acc[r] + value

    by_two((count + 1) // 2, images)


def grad_tap(acc, r, s):
    return (
        acc[r, C * s : C * s + C, 0:C] + acc[r, C * (s + 1) : C * (s + 1) + C, C : 2 * C]
    )


def statistics(count, z, cells, tiles, chunk, blocks, summed=None):
    def add(i, acc):
        for start in range(0, tiles, chunk):
            for m in range(blocks):
                acc = acc + total(get(z, i, start, chunk, m))
        return acc

    zero = jnp.zeros((8, C), F32)
    mean = channel(loop(count, add, zero) if summed is None else summed) / cells

    def add_square(i, acc):
        for start in range(0, tiles, chunk):
            for m in range(blocks):
                centred = get(z, i, start, chunk, m) - mean
                set_(z, i, start, chunk, m, centred)
                acc = acc + total(centred * centred)
        return acc

    variance = channel(loop(count, add_square, zero)) / cells
    return lax.rsqrt(variance + EPSILON)


def activate(count, zc, s1, s2, pools, inverse, gain, shift, tiles, chunk, blocks, emit):
    scale, offset = 0.5 * gain * inverse, 0.5 * shift

    def step(i, _):
        for start in range(0, tiles, chunk):
            for half in range(blocks // 2):
                sums = []
                for m in (2 * half, 2 * half + 1):
                    centred = get(zc, i, start, chunk, m)
                    h = centred * scale + offset
                    bend = jnp.tanh(h)
                    over, under = 1.0 + bend, 1.0 - bend
                    slope = over * (1.0 + h * under)
                    set_(s1, i, start, chunk, m, slope)
                    if s2 is not None:
                        set_(s2, i, start, chunk, m, over * under * (1.0 - h * bend))
                    sums.append([jnp.sum(v, axis=1) for v in (h * over, slope, slope * centred)])
                pooled, *slopes = (one + two for one, two in zip(*sums))
                for ref, value in zip(pools, slopes):
                    place = i, slice(start // 2, start // 2 + chunk // 2), slice(None), slice(C * half, C * half + C)
                    ref[place] = value.reshape(chunk // 2, 16, C)
                emit(i, start, half, pooled)
        return 0

    loop(count, step)


def pooled_sums(count, pools, up, tiles, blocks):
    def add(i, carry):
        sums = list(carry)
        for half in range(blocks // 2):
            weight = up(i, 0, half, tiles).reshape(tiles // 2, 2, 8, C)
            for n, ref in enumerate(pools):
                value = ref[i, :, :, C * half : C * half + C].reshape(tiles // 2, 2, 8, C)
                sums[n] = sums[n] + total(weight * value)
        return tuple(sums)

    zero = jnp.zeros((8, C), F32)
    return tuple(channel(v) for v in loop(count, add, (zero, zero)))


def first_backward(count, zc, s1, pools, up, dst, gain, inverse, cells, tiles, chunk, blocks):
    one, two = pooled_sums(count, pools, up, tiles, blocks)
    two = two * inverse
    mean_one, mean_two = one / cells, two / cells
    scale = gain * inverse
    offset, tilt = scale * mean_one, scale * mean_two * inverse

    def step(i, _):
        for start in range(0, tiles, chunk):
            for m in range(blocks):
                dy = scale * up(i, start, m // 2, chunk) * get(s1, i, start, chunk, m)
                dz = dy - offset - get(zc, i, start, chunk, m) * tilt
                put(dst, i, start, tiles, m, blocks, dz.reshape(-1, 8, C))
        return 0

    loop(count, step)
    return mean_one, mean_two, one, two


def clear_odd(count, buffers):
    @pl.when(count % 2 == 1)
    def _():
        for buf in buffers:
            buf[count] = jnp.zeros(buf.shape[1:], buf.dtype)


def mix_taps(weight, src, dst):
    for g in range(0, C, MIX_ROWS):
        rows = slice(g, g + MIX_ROWS)
        values = [src(f, rows) for f in range(9)]
        for q in range(9):
            acc = weight(q, 0) * values[0]
            for f in range(1, 9):
                acc = acc + weight(q, f) * values[f]
            dst(q, rows, acc)


def transform(acc, kernel, outer, inner, taps, g_low, t_one, t_two, fast):
    for f in range(9):
        g_low[:, C * f : C * f + C] = grad_tap(acc, f // 3, f % 3).astype(BF16)
    t_one[...] = dot(inner[...].astype(BF16), g_low[...])

    def write(q, rows, value):
        t_two[q, rows, :] = value

    mix_taps(
        lambda q, f: taps[q, f], lambda f, rows: t_one[rows, C * f : C * f + C], write
    )
    turned = dot(t_two[...].reshape(9 * C, C).astype(BF16), outer[...].astype(BF16), NT)
    fast[...] = kernel[...] - STEP_RATE * turned.reshape(9, C, C)


def transform_back(acc, outer, inner, taps, g_low, t_one, t_two, d_low, e, w, payload, u):
    for q in range(9):
        grad = grad_tap(acc, q // 3, q % 3)
        payload[C * q : C * q + C, :] = grad
        d_low[C * q : C * q + C, :] = (-STEP_RATE * grad).astype(BF16)
    e[...] = dot(d_low[...], outer[...].astype(BF16)).reshape(9, C, C)
    payload[AT_OUTER:AT_INNER, :] = dot(
        d_low[...], t_two[...].reshape(9 * C, C).astype(BF16), TN
    )

    def write(f, rows, value):
        w[rows, C * f : C * f + C] = value

    mix_taps(lambda f, q: taps[q, f], lambda q, rows: e[q, rows, :], write)
    w_low = w[...].astype(BF16)
    payload[AT_INNER:AT_SMALL, :] = dot(w_low, g_low[...], NT)
    u[...] = dot(inner[...].astype(BF16), w_low, TN)
    sums = []
    for first in range(0, 9, 3):
        parts = [jnp.zeros((8, C), F32)] * 27
        for g in range(0, C, 8):
            ones = [t_one[g : g + 8, C * f : C * f + C] for f in range(9)]
            for n in range(27):
                if n % 9 == 0:
                    grad = e[first + n // 9, g : g + 8, :]
                parts[n] = parts[n] + grad * ones[n % 9]
        sums += parts
    sums = jnp.concatenate([jnp.sum(v, axis=0, keepdims=True) for v in sums], 0)
    sums = jnp.concatenate([jnp.sum(sums, axis=1, keepdims=True), jnp.zeros((7, 1), F32)], 0)
    spread = jnp.broadcast_to(sums, (88, C))
    row = lax.broadcasted_iota(jnp.int32, (88, C), 0)
    lane = lax.broadcasted_iota(jnp.int32, (88, C), 1)
    spread = jnp.where(row % 9 == lane, spread, 0.0)
    chosen = lax.broadcasted_iota(jnp.int32, (16, 88), 1) // 9 == lax.broadcasted_iota(
        jnp.int32, (16, 88), 0
    )
    payload[AT_SMALL : AT_SMALL + 16, :] = lax.dot_general(
        chosen.astype(F32), spread, NN, precision=lax.Precision.HIGHEST, preferred_element_type=F32
    )


def second_sums(count, c, zc, s1, up, inverse, cells, tiles, chunk, blocks):
    def add(i, carry):
        one, two, three = carry
        for start in range(0, tiles, chunk):
            for m in range(blocks):
                value = get(c, i, start, chunk, m)
                dy = up(i, start, m // 2, chunk) * get(s1, i, start, chunk, m)
                one = one + total(value)
                two = two + total(value * get(zc, i, start, chunk, m))
                three = three + total(value * dy)
        return one, two, three

    zero = jnp.zeros((8, C), F32)
    one, two, three = loop(count, add, (zero, zero, zero))
    return channel(one) / cells, channel(two) * inverse / cells, channel(three) / cells


def second_turn(count, c, zc, s1, s2, up, means, gain, inverse, emit, tiles, chunk, blocks):
    mean_c, mean_cz, _ = means
    scale, tilt = gain * inverse, mean_cz * inverse

    def step(i, carry):
        one, two = carry
        for start in range(0, tiles, chunk):
            for half in range(blocks // 2):
                pooled = None
                weight = scale * up(i, start, half, chunk)
                for m in (2 * half, 2 * half + 1):
                    centred = get(zc, i, start, chunk, m)
                    turned = get(c, i, start, chunk, m) - mean_c - centred * tilt
                    cy = turned * (weight * get(s2, i, start, chunk, m))
                    set_(s2, i, start, chunk, m, cy)
                    one = one + total(cy)
                    two = two + total(cy * centred)
                    if emit is not None:
                        part = jnp.sum(turned * get(s1, i, start, chunk, m), axis=1)
                        pooled = part if pooled is None else pooled + part
                if emit is not None:
                    emit(i, start, half, 0.5 * scale * pooled)
        return one, two

    zero = jnp.zeros((8, C), F32)
    one, two = loop(count, step, (zero, zero))
    return channel(one), channel(two) * inverse


def second_close(
    count, c, zc, s1, t_buf, up, extra, dst, means, sums, first_means, gain, inverse, cells, tiles, chunk, blocks
):
    mean_c, mean_cz, mean_cdy = means
    mean_dy, mean_dyz = first_means
    mean_cy, mean_cyz = sums[0] / cells, sums[1] / cells
    scale = gain * inverse
    mean_cw = mean_cdy - mean_c * mean_dy - mean_cz * mean_dyz
    mean_z = gain * mean_cy - scale * (mean_c * mean_dyz + mean_dy * mean_cz)
    mean_zz = gain * mean_cyz - 2.0 * scale * mean_cz * mean_dyz
    alpha = inverse * gain
    beta = scale * inverse * mean_dyz
    gamma = scale * inverse * mean_cz
    delta = inverse * mean_z
    epsilon = inverse * inverse * (mean_zz + scale * mean_cw)

    def step(i, _):
        for start in range(0, tiles, chunk):
            for m in range(blocks):
                weight = -gamma * up(i, start, m // 2, chunk)
                if extra is not None:
                    weight = weight + alpha * extra(i, start, m // 2, chunk)
                value = (
                    alpha * get(t_buf, i, start, chunk, m)
                    + weight * get(s1, i, start, chunk, m)
                    - beta * get(c, i, start, chunk, m)
                    - epsilon * get(zc, i, start, chunk, m)
                    - delta
                )
                put(dst, i, start, tiles, m, blocks, value.reshape(-1, 8, C))
        return 0

    loop(count, step)
    return sums[1] + inverse * cells * mean_cw


def image_grads(count, pairs, dst, wide):
    def emit(i, q, value):
        for o in range(2):
            v = value[:, C * o : C * o + C].reshape(16, 2, 8, C)
            for b in range(2):
                wide[16 * b : 16 * b + 16, pl.ds(2 * q + o, 8, stride=4), :] = v[:, b]
        if q == 1:
            dst[i] = wide[...].astype(BF16)

    conv_one(count, pairs, emit, NT)

    def dead(i, _):
        dst[i] = jnp.zeros(dst.shape[1:], BF16)
        return 0

    lax.fori_loop(count, dst.shape[0], dead, 0)


def query_grad_kernel(count, grads, weights, after, dst, zeros, wide):
    zeros[...] = jnp.zeros(zeros.shape, F32)
    image_grads(count[0], [(grads, weights)], dst, wide)


def support_grad_kernel(
    count, inner_grads, inner_weights, grads, kernel, after, dst, zeros, wide, weights
):
    zeros[...] = jnp.zeros(zeros.shape, F32)
    write_weights_back(weights, lambda r, s: kernel[3 * r + s])
    image_grads(count[0], [(inner_grads, inner_weights), (grads, weights)], dst, wide)


def run_image_grads(kernel, name, shape, after, operands, scratch):
    vmem = pl.BlockSpec(memory_space=pltpu.VMEM)
    images = operands[1].shape[0]
    convs = (len(operands) - 1) // 2
    return pl.pallas_call(
        kernel,
        out_shape=(jax.ShapeDtypeStruct(shape, BF16), pltpu.VMEM((8, C), F32)),
        in_specs=[pl.BlockSpec(memory_space=pltpu.SMEM)]
        + [vmem] * (len(operands) - 1)
        + [pl.BlockSpec(memory_space=pl.ANY)],
        out_specs=(vmem, vmem),
        scratch_shapes=[pltpu.VMEM((32, 32, C), F32)] + scratch,
        compiler_params=pltpu.CompilerParams(vmem_limit_bytes=VMEM_SMALL),
        cost_estimate=pl.CostEstimate(
            flops=2 * images * convs * 1024 * 1536 * C,
            bytes_accessed=images * (convs + 1) * 32 * 32 * C * 2,
            transcendentals=0,
        ),
        name=name,
    )(*operands, after)


SCALARS = ["support_count", "query_count", "taps_one", "taps_two"]
NORMS = ["gain_one", "shift_one", "gain_two", "shift_two"]
AT_OUTER, AT_INNER, AT_SMALL, AT_GAIN, HALF_ROWS = 9 * C, 10 * C, 11 * C, 11 * C + 16, 11 * C + 32
QUARTER = HALF_ROWS // 4
FETCHED = [
    "kernel_one",
    "support",
    "gain_one",
    "shift_one",
    "gain_two",
    "shift_two",
    "kernel_two",
    "target",
    "inner_two",
    "outer_two",
    "inner_one",
    "outer_one",
    "query",
    "cotangent",
]
HELD = ["query_output", "grad_q", "back_q", "grad_s", "back_s", "grad_e"]
KEPT = [f"keep_{at}" for at in range(4)]
GIVEN = [f"send_{at}" for at in range(4)]


def scratch_of(s_cap, q_cap):
    def operand(count, tiles, blocks):
        return pltpu.VMEM((count, tiles + 2, 16, C * (blocks + 2)), BF16)

    def plain(count, tiles, blocks):
        return pltpu.VMEM((count, tiles, 16, C * blocks), F32)

    weights = pltpu.VMEM((1536, 256), BF16)
    weights_back = pltpu.VMEM((256, 1536), BF16)
    square = pltpu.VMEM((C, 9 * C), F32)
    square_low = pltpu.VMEM((C, 9 * C), BF16)
    stack = pltpu.VMEM((9, C, C), F32)
    s_even, q_even = s_cap + s_cap % 2, q_cap + q_cap % 2
    return dict(
        wide=pltpu.VMEM((32, 32, C), F32),
        xs=operand(s_cap, 16, 4),
        xq=operand(q_cap, 16, 4),
        ds=operand(s_cap, 16, 4),
        dq=operand(q_cap, 16, 4),
        zs=plain(s_cap, 16, 4),
        s1s=plain(s_cap, 16, 4),
        s2s=plain(s_cap, 16, 4),
        zq=plain(q_cap, 16, 4),
        s1q=plain(q_cap, 16, 4),
        hs=operand(s_even, 8, 2),
        ds2=operand(s_even, 8, 2),
        hq=operand(q_even, 8, 2),
        dq2=operand(q_even, 8, 2),
        zs2=plain(s_even, 8, 2),
        s1s2=plain(s_even, 8, 2),
        s2s2=plain(s_even, 8, 2),
        dhs=plain(s_even, 8, 2),
        chs_back=plain(s_even, 8, 2),
        zq2=plain(q_even, 8, 2),
        s1q2=plain(q_even, 8, 2),
        dhq=plain(q_even, 8, 2),
        p1s=plain(s_cap, 8, 2),
        p2s=plain(s_cap, 8, 2),
        p1s2=plain(s_cap, 4, 1),
        p2s2=plain(s_cap, 4, 1),
        p1q=plain(q_cap, 8, 2),
        p2q=plain(q_cap, 8, 2),
        p1q2=plain(q_cap, 4, 1),
        p2q2=plain(q_cap, 4, 1),
        sums=pltpu.VMEM((3, 8, C), F32),
        w_a=weights,
        w_b=weights,
        w_c=weights,
        b_k2=weights_back,
        b_f1=weights_back,
        b_f2=weights_back,
        b_u1=weights_back,
        b_u2=weights_back,
        acc=pltpu.VMEM((3, 512, 256), F32),
        g_one=square_low,
        g_two=square_low,
        t1_one=square,
        t1_two=square,
        t2_one=stack,
        t2_two=stack,
        f_one=stack,
        f_two=stack,
        d_low=pltpu.VMEM((9 * C, C), BF16),
        e_buf=stack,
        w_buf=square,
        u_buf=square,
        payload=pltpu.VMEM((2, HALF_ROWS, C), F32),
        gain_one_v=pltpu.VMEM((1, C), F32),
        shift_one_v=pltpu.VMEM((1, C), F32),
        gain_two_v=pltpu.VMEM((1, C), F32),
        shift_two_v=pltpu.VMEM((1, C), F32),
        output_v=pltpu.VMEM((q_cap, 8, 8, C), BF16),
        support_v=pltpu.VMEM((s_cap, 32, 32, C), BF16),
        query_v=pltpu.VMEM((q_cap, 32, 32, C), BF16),
        target_v=pltpu.VMEM((s_cap, 8, 8, C), BF16),
        cotangent_v=pltpu.VMEM((q_cap, 8, 8, C), BF16),
        kernel_one_v=stack,
        kernel_two_v=stack,
        inner_one_v=pltpu.VMEM((C, C), F32),
        outer_one_v=pltpu.VMEM((C, C), F32),
        inner_two_v=pltpu.VMEM((C, C), F32),
        outer_two_v=pltpu.VMEM((C, C), F32),
        fetch_sem=pltpu.SemaphoreType.DMA((len(FETCHED),)),
        send_sem=pltpu.SemaphoreType.DMA((len(HELD),)),
    )


def task_kernel(names, *refs):
    k = SimpleNamespace(**dict(zip(names, refs)))
    fetches = {}
    for n, name in enumerate(FETCHED):
        fetches[name] = pltpu.make_async_copy(getattr(k, name), getattr(k, name + "_v"), k.fetch_sem.at[n])
        setattr(k, name, getattr(k, name + "_v"))
    for name in FETCHED[:6]:
        fetches[name].start()
    sent = []

    def ready(*wanted):
        for name in wanted:
            fetches[name].wait()

    def send(name, source):
        copy = pltpu.make_async_copy(source, getattr(k, name), k.send_sem.at[HELD.index(name)])
        copy.start()
        sent.append(copy)

    def close_layer(layer, gain_grad, shift_grad):
        pay = k.payload.at[layer]
        pay[AT_GAIN : AT_GAIN + 2, :] = jnp.concatenate([gain_grad[0:1], shift_grad[0:1]], 0)
        pay[AT_GAIN + 2 :, :] = jnp.zeros((HALF_ROWS - AT_GAIN - 2, C), F32)
        half, place = my_place()
        for at in range(4):
            rows = pl.ds(pl.multiple_of((place ^ at) * QUARTER, 8), QUARTER)
            for kept in (True, False):
                target = getattr(k, f"keep_{at}" if kept else f"send_{at}")

                @pl.when(half == (layer if kept else 1 - layer))
                def _(target=target, rows=rows):
                    target[...] = pay[rows, :]

    ns, nq = k.support_count[0], k.query_count[0]
    ns_f, nq_f = ns.astype(F32), nq.astype(F32)
    pay_one, pay_two = k.payload.at[0], k.payload.at[1]
    k.cs, k.es, k.cs2, k.es2, k.chs = k.zq, k.xq, k.zq2, k.hq, k.dq2
    one = dict(tiles=16, chunk=4, blocks=4)
    two = dict(tiles=8, chunk=4, blocks=2)
    wide = k.wide

    def load_images(count, src, dst):
        def image(i, _):
            wide[...] = src[i].astype(F32)
            for m in range(4):
                v = wide[:, pl.ds(m, 8, stride=4), :].reshape(2, 16, 1, 8, C)
                v = jnp.concatenate([v[0], v[1]], 1)
                put(dst, i, 0, 16, m, 4, v.reshape(32, 8, C))
            return 0

        loop(count, image)

    def keep(dst, terms):
        k.sums[...] = jnp.zeros(k.sums.shape, F32)

        def emit(i, q, value):
            dst[i, :, :, 256 * q : 256 * q + 256] = value.reshape(16, 16, 256)
            added = None
            for o in range(2):
                block = value[:, C * o : C * o + C].reshape(8, 2, 2, 8, C)
                parts = [total(term) for term in terms(i, 2 * q + o, block)]
                added = parts if added is None else [v + w for v, w in zip(added, parts)]
            for n, part in enumerate(added):
                k.sums[n] += part

        return emit

    def alone(i, m, block):
        return [block]

    def pool_to(dst):
        def emit(i, start, half, pooled):
            put(dst, i, start // 2, 8, half, 2, (0.25 * pooled).reshape(-1, 8, C))

        return emit

    def up_from(ref):
        def up(i, start, half, chunk):
            number = chunk // 2
            v = ref[i, start // 2 : start // 2 + number, :, C * half : C * half + C]
            return 0.125 * v.reshape(number, 1, 2, 8, C)

        return up

    def up_from_rows(ref, scale):
        def up(i, start, half, chunk):
            number = chunk // 2
            v = ref[i].astype(F32) * scale
            parts = [v[at : at + number].reshape(number, 1, 1, 8, C) for at in (start // 2, 4 + start // 2)]
            return jnp.concatenate(parts, 2)

        return up

    def tap_of(ref):
        return lambda r, s: ref[3 * r + s]

    def tap_wide(ref):
        return lambda r, s: ref[:, C * (3 * r + s) : C * (3 * r + s) + C]

    pools_one, pools_two = (k.p1s, k.p2s), (k.p1s2, k.p2s2)
    pools_q1, pools_q2 = (k.p1q, k.p2q), (k.p1q2, k.p2q2)

    cells_one, cells_two = ns_f * 1024.0, ns_f * 256.0
    ready("kernel_one")
    write_weights(k.w_a, tap_of(k.kernel_one))
    ready("support", *NORMS)
    for name in FETCHED[6:]:
        fetches[name].start()
    gain_one, shift_one, gain_two, shift_two = (
        jnp.broadcast_to(getattr(k, name)[...], (8, C)) for name in NORMS
    )
    load_images(ns, k.support, k.xs)
    conv_one(ns, [(k.xs, k.w_a)], keep(k.zs, alone))
    stats_one = statistics(ns, k.zs, cells_one, summed=k.sums[0], **one)
    activate(ns, k.zs, k.s1s, k.s2s, pools_one, stats_one, gain_one, shift_one, emit=pool_to(k.hs), **one)
    clear_odd(ns, [k.hs, k.ds2])
    ready("kernel_two", "target", "inner_two", "outer_two")
    write_weights(k.w_b, tap_of(k.kernel_two))
    conv_two(ns, [(k.hs, k.w_b)], k.zs2)
    stats_two = statistics(ns, k.zs2, cells_two, **two)
    activate(ns, k.zs2, k.s1s2, k.s2s2, pools_two, stats_two, gain_two, shift_two, emit=lambda *a: None, **two)

    up_two = up_from_rows(k.target, 1.0 / (512.0 * ns_f))
    mean_dy2, mean_dyz2, _, _ = first_backward(
        ns, k.zs2, k.s1s2, pools_two, up_two, k.ds2, gain_two, stats_two, cells_two, **two
    )
    kernel_grad_two(ns, [(k.hs, k.ds2)], k.acc)
    transform(
        k.acc, k.kernel_two, k.outer_two, k.inner_two, k.taps_two, k.g_two, k.t1_two, k.t2_two, k.f_two
    )
    write_weights_back(k.b_k2, tap_of(k.kernel_two))
    conv_two(ns, [(k.ds2, k.b_k2)], k.dhs, NT)
    up_one = up_from(k.dhs)
    mean_dy1, mean_dyz1, _, _ = first_backward(
        ns, k.zs, k.s1s, pools_one, up_one, k.ds, gain_one, stats_one, cells_one, **one
    )
    send("grad_s", k.ds)
    ready("inner_one", "outer_one", "query", "cotangent")
    kernel_grad_one(ns, k.xs, k.ds, k.acc)
    transform(
        k.acc, k.kernel_one, k.outer_one, k.inner_one, k.taps_one, k.g_one, k.t1_one, k.t2_one, k.f_one
    )

    cells_q1, cells_q2 = nq_f * 1024.0, nq_f * 256.0
    write_weights(k.w_a, tap_of(k.f_one))
    load_images(nq, k.query, k.xq)
    conv_one(nq, [(k.xq, k.w_a)], keep(k.zq, alone))
    stats_q1 = statistics(nq, k.zq, cells_q1, summed=k.sums[0], **one)
    activate(nq, k.zq, k.s1q, None, pools_q1, stats_q1, gain_one, shift_one, emit=pool_to(k.hq), **one)
    clear_odd(nq, [k.hq, k.dq2])
    write_weights(k.w_c, tap_of(k.f_two))
    conv_two(nq, [(k.hq, k.w_c)], k.zq2)
    stats_q2 = statistics(nq, k.zq2, cells_q2, **two)

    def produce(i, start, half, pooled):
        v = (0.25 * pooled).astype(BF16)
        at, number = start // 2, v.shape[0]
        k.output_v[i, at : at + number] = v[:, 0]
        k.output_v[i, 4 + at : 4 + at + number] = v[:, 1]

    activate(nq, k.zq2, k.s1q2, None, pools_q2, stats_q2, gain_two, shift_two, emit=produce, **two)

    def dead(i, _):
        k.output_v[i] = jnp.zeros(k.output_v.shape[1:], BF16)
        return 0

    lax.fori_loop(nq, k.output_v.shape[0], dead, 0)
    send("query_output", k.output_v)

    _, _, db2, dg2 = first_backward(
        nq, k.zq2, k.s1q2, pools_q2, up_from_rows(k.cotangent, 0.125 / nq_f), k.dq2, gain_two, stats_q2, cells_q2, **two
    )
    kernel_grad_two(nq, [(k.hq, k.dq2)], k.acc)
    transform_back(
        k.acc, k.outer_two, k.inner_two, k.taps_two, k.g_two, k.t1_two, k.t2_two, k.d_low, k.e_buf, k.w_buf,
        pay_two, k.u_buf,
    )
    write_weights_back(k.b_f2, tap_of(k.f_two))
    write_weights(k.w_c, tap_wide(k.u_buf))
    write_weights_back(k.b_u2, tap_wide(k.u_buf))
    conv_two(nq, [(k.dq2, k.b_f2)], k.dhq, NT)
    _, _, db1, dg1 = first_backward(
        nq, k.zq, k.s1q, pools_q1, up_from(k.dhq), k.dq, gain_one, stats_q1, cells_q1, **one
    )
    send("grad_q", k.dq)
    kernel_grad_one(nq, k.xq, k.dq, k.acc)
    transform_back(
        k.acc, k.outer_one, k.inner_one, k.taps_one, k.g_one, k.t1_one, k.t2_one, k.d_low, k.e_buf, k.w_buf,
        pay_one, k.u_buf,
    )
    write_weights_back(k.b_f1, tap_of(k.f_one))
    send("back_q", k.b_f1)
    write_weights(k.w_a, tap_wide(k.u_buf))
    write_weights_back(k.b_u1, tap_wide(k.u_buf))
    send("back_s", k.b_u1)

    clear_odd(ns, [k.chs, k.es2])

    def second_terms(i, m, block):
        dy = up_one(i, 0, m // 2, 16) * get(k.s1s, i, 0, 16, m)
        return [block, block * get(k.zs, i, 0, 16, m), block * dy]

    conv_one(ns, [(k.xs, k.w_a)], keep(k.cs, second_terms))
    means_one = tuple(channel(k.sums[n]) / cells_one for n in range(3))
    means_one = means_one[0], means_one[1] * stats_one, means_one[2]
    turn_one = second_turn(
        ns, k.cs, k.zs, k.s1s, k.s2s, up_one, means_one, gain_one, stats_one, pool_to(k.chs), **one
    )
    conv_two(ns, [(k.chs, k.w_b), (k.hs, k.w_c)], k.cs2)
    means_two = second_sums(ns, k.cs2, k.zs2, k.s1s2, up_two, stats_two, cells_two, **two)
    turn_two = second_turn(
        ns, k.cs2, k.zs2, k.s1s2, k.s2s2, up_two, means_two, gain_two, stats_two, None, **two
    )
    extra_g2 = second_close(
        ns, k.cs2, k.zs2, k.s1s2, k.s2s2, up_two, None, k.es2, means_two, turn_two, (mean_dy2, mean_dyz2),
        gain_two, stats_two, cells_two, **two,
    )
    conv_two(ns, [(k.ds2, k.b_u2), (k.es2, k.b_k2)], k.chs_back, NT)
    kernel_grad_two(ns, [(k.chs, k.ds2), (k.hs, k.es2)], k.acc)
    for f in range(9):
        pay_two[C * f : C * f + C, :] += grad_tap(k.acc, f // 3, f % 3)
    close_layer(1, dg2 + extra_g2, db2 + turn_two[0])
    up_back = up_from(k.chs_back)
    more = pooled_sums(ns, pools_one, up_back, 16, 4)
    turn_one = (turn_one[0] + more[0], turn_one[1] + more[1] * stats_one)
    extra_g1 = second_close(
        ns, k.cs, k.zs, k.s1s, k.s2s, up_one, up_back, k.es, means_one, turn_one, (mean_dy1, mean_dyz1),
        gain_one, stats_one, cells_one, **one,
    )
    send("grad_e", k.es.at[pl.ds(0, k.xs.shape[0])])
    kernel_grad_one(ns, k.xs, k.es, k.acc)
    for f in range(9):
        pay_one[C * f : C * f + C, :] += grad_tap(k.acc, f // 3, f % 3)
    close_layer(0, dg1 + extra_g1, db1 + turn_one[0])
    for copy in sent:
        copy.wait()


def run_task(values):
    s_cap, q_cap = values["support"].shape[0], values["query"].shape[0]
    scratch = scratch_of(s_cap, q_cap)
    vmem = pl.BlockSpec(memory_space=pltpu.VMEM)
    smem = pl.BlockSpec(memory_space=pltpu.SMEM)
    anywhere = pl.BlockSpec(memory_space=pl.ANY)

    def operand(count):
        return jax.ShapeDtypeStruct((count, 18, 16, 6 * C), BF16)

    back = jax.ShapeDtypeStruct((256, 1536), BF16)
    rows = pltpu.VMEM((QUARTER, C), F32)
    inputs = SCALARS + FETCHED
    outputs = HELD + KEPT + GIVEN
    results = pl.pallas_call(
        partial(task_kernel, inputs + outputs + list(scratch)),
        out_shape=(
            jax.ShapeDtypeStruct(values["cotangent"].shape, BF16),
            operand(q_cap),
            back,
            operand(s_cap),
            back,
            operand(s_cap),
            *[rows] * 8,
        ),
        in_specs=[smem] * len(SCALARS) + [anywhere] * len(FETCHED),
        out_specs=[anywhere] * len(HELD) + [vmem] * 8,
        scratch_shapes=list(scratch.values()),
        compiler_params=pltpu.CompilerParams(vmem_limit_bytes=VMEM_BYTES),
        name="task",
    )(*[values[name] for name in inputs])
    return dict(zip(outputs, results))


def swap(value, mask):
    extent = lax.axis_size(AXES)
    return lax.ppermute(value, AXES, [(place, place ^ mask) for place in range(extent)])


def sum_quarters(kept, sent, first, second):
    extent = lax.axis_size(AXES)
    come = {n: swap(sent[n], 1) for n in (3, 1, 2, 0)}
    mine = {n: kept[n] + come[n] for n in (3, 1, 2, 0)}
    terms = {n: swap(mine[n], 2 * n) for n in (3, 1, 2)}
    one, zeros = first(come[0][0:8])
    part = mine[0] + terms[3] + terms[1] + terms[2] + zeros[0:1]
    mask, two = 8, None
    while mask < extent:
        passed = swap(part, mask)
        if 2 * mask >= extent:
            two, zeros = second(part[0:8])
            passed = passed + zeros[0:1]
        part = part + passed
        mask *= 2
    if two is None:
        two, _ = second(part[0:8])
    quarters = [part] + [swap(part, 2 * n) for n in (1, 2, 3)]
    return one, two, quarters, [swap(quarter, 1) for quarter in quarters]


def sum_plain(kept, sent, first, second):
    half, at = my_place()
    whole = jnp.stack([*kept, *sent]).reshape(2, 4, QUARTER, C)
    whole = jnp.where(half == 0, whole, whole[::-1])
    order = at ^ jnp.arange(4)
    whole = lax.psum(jnp.take(whole, order, axis=1), AXES)
    whole = jnp.take(jnp.where(half == 0, whole, whole[::-1]), order, axis=1)
    results = first(whole)[0], second(whole)[0]
    return *results, list(whole[0]), list(whole[1])


LAYER = ["outer", "inner", "taps"]


def my_place():
    me = lax.axis_index(AXES)
    return me & 1, (me >> 1) & 3


def finish_kernel(*refs):
    pieces, refs = refs[:8], refs[8:]
    factors, refs = refs[:6], refs[6:]
    results, refs = refs[:12], refs[12:]
    rest, kernel_sem = refs
    half, at = my_place()
    whole = AT_OUTER // QUARTER
    last = AT_OUTER - whole * QUARTER
    for n, piece in enumerate(pieces):
        quarter = at ^ (n % 4)
        for layer in range(2):
            kernel = results[6 * layer]
            own = half == layer if n < 4 else half != layer

            @pl.when(own & (quarter < whole))
            def _(piece=piece, kernel=kernel, quarter=quarter, layer=layer):
                start = pl.multiple_of(quarter * QUARTER, 8)
                pltpu.make_async_copy(
                    piece, kernel.at[pl.ds(start, QUARTER)], kernel_sem.at[layer]
                ).start()

            @pl.when(own & (quarter == whole))
            def _(piece=piece, kernel=kernel, layer=layer):
                rest[layer] = piece[last:QUARTER, :]
                pltpu.make_async_copy(
                    piece.at[pl.ds(0, last)], kernel.at[pl.ds(whole * QUARTER, last)], kernel_sem.at[layer]
                ).start()

    for layer in range(2):
        kernel, gain, shift, outer, inner, taps = results[6 * layer : 6 * layer + 6]
        base = AT_GAIN - AT_OUTER
        gain[...] = rest[layer, base : base + 1, :]
        shift[...] = rest[layer, base + 1 : base + 2, :]
        for start, size, factor, result in zip(
            (0, C, 2 * C), (C, C, 9), factors[3 * layer : 3 * layer + 3], (outer, inner, taps)
        ):
            row = lax.broadcasted_iota(jnp.int32, (size, size), 0)
            column = lax.broadcasted_iota(jnp.int32, (size, size), 1)
            unit = jnp.where(row == column, 1.0, 0.0)
            value = rest[layer, start : start + size, :size]
            result[...] = value + 2.0 * PENALTY * (factor[...] - unit)
    for layer in range(2):
        kernel = results[6 * layer]
        pltpu.make_async_copy(kernel, kernel, kernel_sem.at[layer]).wait()


def run_finish(pieces, factors):
    vmem = pl.BlockSpec(memory_space=pltpu.VMEM)
    anywhere = pl.BlockSpec(memory_space=pl.ANY)

    def shape(*dims):
        return jax.ShapeDtypeStruct(dims, F32)

    layer = [shape(9 * C, C), shape(1, C), shape(1, C), shape(C, C), shape(C, C), shape(9, 9)]
    return pl.pallas_call(
        finish_kernel,
        out_shape=layer * 2,
        in_specs=[vmem] * 14,
        out_specs=([anywhere] + [vmem] * 5) * 2,
        scratch_shapes=[
            pltpu.VMEM((2, HALF_ROWS - AT_OUTER, C), F32),
            pltpu.SemaphoreType.DMA((2,)),
        ],
        compiler_params=pltpu.CompilerParams(vmem_limit_bytes=VMEM_SMALL),
        name="finish",
    )(*pieces, *factors)


def body(
    support_images,
    query_images,
    support_target,
    query_cotangent,
    support_count,
    query_count,
    kernel_one,
    kernel_two,
    gain_one,
    shift_one,
    gain_two,
    shift_two,
    outer_one,
    inner_one,
    taps_one,
    outer_two,
    inner_two,
    taps_two,
):
    shared = dict(
        taps_one=taps_one,
        taps_two=taps_two,
        kernel_one=kernel_one.reshape(9, C, C),
        kernel_two=kernel_two.reshape(9, C, C),
        gain_one=gain_one.reshape(1, C),
        shift_one=shift_one.reshape(1, C),
        gain_two=gain_two.reshape(1, C),
        shift_two=shift_two.reshape(1, C),
        outer_one=outer_one,
        inner_one=inner_one,
        outer_two=outer_two,
        inner_two=inner_two,
    )
    tasks = range(support_images.shape[0])
    results = [
        run_task(
            dict(
                shared,
                support_count=support_count[task : task + 1],
                query_count=query_count[task : task + 1],
                support=support_images[task],
                query=query_images[task],
                target=support_target[task],
                cotangent=query_cotangent[task],
            )
        )
        for task in tasks
    ]

    def query_grads(after):
        done = [
            run_image_grads(
                query_grad_kernel,
                "query_grad",
                query_images.shape[1:],
                after,
                [query_count[task : task + 1], results[task]["grad_q"], results[task]["back_q"]],
                [],
            )
            for task in tasks
        ]
        return jnp.stack([value for value, _ in done]), sum(zeros for _, zeros in done)

    def support_grads(after):
        done = [
            run_image_grads(
                support_grad_kernel,
                "support_grad",
                support_images.shape[1:],
                after,
                [
                    support_count[task : task + 1],
                    *[results[task][name] for name in ("grad_s", "back_s", "grad_e")],
                    shared["kernel_one"],
                ],
                [pltpu.VMEM((256, 1536), BF16)],
            )
            for task in tasks
        ]
        return jnp.stack([value for value, _ in done]), sum(zeros for _, zeros in done)

    kept = [sum(result[name] for result in results) for name in KEPT]
    sent = [sum(result[name] for result in results) for name in GIVEN]
    extent = lax.axis_size(AXES)
    if extent < 8 or extent & (extent - 1):
        summed = sum_plain(kept, sent, query_grads, support_grads)
    else:
        summed = sum_quarters(kept, sent, query_grads, support_grads)
    query_grad, support_grad, mine, others = summed
    factors = [outer_one, inner_one, taps_one, outer_two, inner_two, taps_two]
    last = run_finish([*mine, *others], factors)
    return (
        jnp.stack([result["query_output"] for result in results]),
        support_grad,
        query_grad,
        last[0].reshape(3, 3, C, C),
        last[6].reshape(3, 3, C, C),
        *[last[at].reshape(C) for at in (1, 2, 7, 8)],
        *last[3:6],
        *last[9:12],
    )


def solution(mesh):
    split = P(("tasks", "group"))
    return jax.shard_map(
        body,
        mesh=mesh,
        in_specs=(split,) * 6 + (P(),) * 12,
        out_specs=(split,) * 3 + (P(),) * 12,
        check_vma=False,
    )
```

profile of v0, /device:TPU:0, one launch (start us, length us, event | category | flops | bytes accessed | tf_op | source)
XLA Modules:
  0.0 85.8 jit_solution(13971359565252066753)
XLA Ops:
  1.9 29.9 %task.1 = (bf16[6,8,8,128]{3,2,1,0:T(8,128)(2,1)}, bf16[6,18,16,768]{3,2,1,0:T(8,128)(2,1)}, bf16[256,1536]{1,0:T(8,128)(2,1)}, bf16[4,18,16,768]{3,2,1,0:T(8,12...) custom-call(s32[1]{0:T(128)S(6)} %copy.33.refs_0_.count, ...), custom_call_target="tpu_custom_call" | custom-call | tf_op jit(solution)/shard_map/task/pallas_call | solution.py:858
  31.8 0.1 collective-permute-start.5
  31.9 0.5 collective-permute-start.3
  32.4 0.1 collective-permute-start.1
  32.5 0.4 collective-permute-start
  32.9 0.4 collective-permute-done.5
  33.3 4.2 %collective-permute-start.6 = (f32[360,128]{1,0:T(8,128)S(1)}, f32[360,128]{1,0:T(8,128)S(1)}, u32[]{:S(2)}, u32[]{:S(2)}) collective-permute-start(f32[360,128]{1,0:T(8,128)S(1)} %add.52), channel_id=1, source_target_pairs={{0,4},{1,5},{2,6},{3,7},{4,0},{5,1},{6,2},{7,3},{8,12},{9,13},{10,... | collective-permute-start | bytes 552968 | tf_op jit(solution)/shard_map/ppermute | solution.py:880
  37.6 2.6 %collective-permute-start.4 = (f32[360,128]{1,0:T(8,128)S(1)}, f32[360,128]{1,0:T(8,128)S(1)}, u32[]{:S(2)}, u32[]{:S(2)}) collective-permute-start(f32[360,128]{1,0:T(8,128)S(1)} %add.50), channel_id=1, source_target_pairs={{0,2},{1,3},{2,0},{3,1},{4,6},{5,7},{6,4},{7,5},{8,10},{9,11},{10,... | collective-permute-start | bytes 552968 | tf_op jit(solution)/shard_map/ppermute | solution.py:880
  40.2 0.1 collective-permute-start.2
  40.3 1.7 %copy-done.7 = bf16[6,18,16,768]{3,2,1,0:T(8,128)(2,1)S(1)} copy-done((bf16[6,18,16,768]{3,2,1,0:T(8,128)(2,1)S(1)}, bf16[6,18,16,768]{3,2,1,0:T(8,128)(2,1)}, u32[]{:S(2)}) %copy-start.7) | copy-done | bytes 2654232
  42.1 1.1 %copy-done.11 = bf16[256,1536]{1,0:T(8,128)(2,1)S(1)} copy-done((bf16[256,1536]{1,0:T(8,128)(2,1)S(1)}, bf16[256,1536]{1,0:T(8,128)(2,1)}, u32[]{:S(2)}) %copy-start.11) | copy-done | bytes 786456
  43.2 4.0 %query_grad.1 = (bf16[6,32,32,128]{3,2,1,0:T(8,128)(2,1)}, f32[8,128]{1,0:T(8,128)S(1)}) custom-call(s32[1]{0:T(128)S(6)} %copy.34.refs_1_.count, bf16[6,18,16,768]{3,2,1,0:T(8,128)(2,1)S(1)} %copy-done.7, bf16[256,1536]{1,0:T(8,128)(2,1)S(1)} %copy-done.11, f32[8,128]{1,0:T(8,128)S(1)} %slice.16.after), custom_call_target="tpu_custom_call" | custom-call | flops 2415919104 | bytes 3145728 | tf_op jit(solution)/shard_map/query_grad/pallas_call | solution.py:476
  47.2 1.8 %collective-permute-done.4 = f32[360,128]{1,0:T(8,128)S(1)} collective-permute-done((f32[360,128]{1,0:T(8,128)S(1)}, f32[360,128]{1,0:T(8,128)S(1)}, u32[]{:S(2)}, u32[]{:S(2)}) %collective-permute-start.4) | collective-permute-done | bytes 184352 | tf_op jit(solution)/shard_map/ppermute | solution.py:880
  49.0 0.1 add_add_fusion.1
  49.1 6.6 %collective-permute-start.7 = (f32[360,128]{1,0:T(8,128)S(1)}, f32[360,128]{1,0:T(8,128)S(1)}, u32[]{:S(2)}, u32[]{:S(2)}) collective-permute-start(f32[360,128]{1,0:T(8,128)S(1)} %add_add_fusion.1), channel_id=1, source_target_pairs={{0,8},{1,9},{2,10},{3,11},{4,12},{5,13},{6,14},{7,15},{8,0},{9,1},... | collective-permute-start | bytes 552968 | tf_op jit(solution)/shard_map/ppermute | solution.py:880
  55.7 4.1 %collective-permute-done.7 = f32[360,128]{1,0:T(8,128)S(1)} collective-permute-done((f32[360,128]{1,0:T(8,128)S(1)}, f32[360,128]{1,0:T(8,128)S(1)}, u32[]{:S(2)}, u32[]{:S(2)}) %collective-permute-start.7) | collective-permute-done | bytes 184352 | tf_op jit(solution)/shard_map/ppermute | solution.py:880
  59.8 4.0 %collective-permute-start.8 = (f32[360,128]{1,0:T(8,128)S(1)}, f32[360,128]{1,0:T(8,128)S(1)}, u32[]{:S(2)}, u32[]{:S(2)}) collective-permute-start(f32[360,128]{1,0:T(8,128)S(1)} %add.57), channel_id=1, source_target_pairs={{0,16},{1,17},{2,18},{3,19},{4,20},{5,21},{6,22},{7,23},{8,24},{9,... | collective-permute-start | bytes 552968 | tf_op jit(solution)/shard_map/ppermute | solution.py:880
  63.8 0.0 copy-start.1
  63.8 0.0 copy-start.2
  63.8 0.0 copy-start.3
  63.9 0.0 copy-start.5
  63.9 0.0 copy-start.6
  63.9 3.0 %support_grad.1 = (bf16[4,32,32,128]{3,2,1,0:T(8,128)(2,1)}, f32[8,128]{1,0:T(8,128)S(1)}) custom-call(s32[1]{0:T(128)S(6)} %copy.33.refs_0_.count, bf16[4,18,16,768]{3,2,1,0:T(8,128)(2,1)S(1)} %copy-done.8, bf16[256,1536]{1,0:T(8,128)(2,1)S(1)} %copy-done.10, bf16[4,18,16,768]{3,2,1,0:T(8,128)(2,1)S(1)} %copy-done.9, f32[9,128,128]{2,1,0:T(8,128)S(1)} %bitcast.24, ...), custom_call_target="tpu_custom_call" | custom-call | flops 3221225472 | bytes 3145728 | tf_op jit(solution)/shard_map/support_grad/pallas_call | solution.py:476
  66.9 4.6 %collective-permute-done.8 = f32[360,128]{1,0:T(8,128)S(1)} collective-permute-done((f32[360,128]{1,0:T(8,128)S(1)}, f32[360,128]{1,0:T(8,128)S(1)}, u32[]{:S(2)}, u32[]{:S(2)}) %collective-permute-start.8) | collective-permute-done | bytes 184352 | tf_op jit(solution)/shard_map/ppermute | solution.py:880
  71.5 0.7 collective-permute-start.9
  72.2 1.1 %collective-permute-start.10 = (f32[360,128]{1,0:T(8,128)S(1)}, f32[360,128]{1,0:T(8,128)S(1)}, u32[]{:S(2)}, u32[]{:S(2)}) collective-permute-start(f32[360,128]{1,0:T(8,128)S(1)} %add_add_fusion.refs_0_), channel_id=1, source_target_pairs={{0,4},{1,5},{2,6},{3,7},{4,0},{5,1},{6,2},{7,3},{8,12},{9,13},{10,... | collective-permute-start | bytes 552968 | tf_op jit(solution)/shard_map/ppermute | solution.py:880
  73.3 1.8 %collective-permute-start.11 = (f32[360,128]{1,0:T(8,128)S(1)}, f32[360,128]{1,0:T(8,128)S(1)}, u32[]{:S(2)}, u32[]{:S(2)}) collective-permute-start(f32[360,128]{1,0:T(8,128)S(1)} %add_add_fusion.refs_0_), channel_id=1, source_target_pairs={{0,6},{1,7},{2,4},{3,5},{4,2},{5,3},{6,0},{7,1},{8,14},{9,15},{10,... | collective-permute-start | bytes 552968 | tf_op jit(solution)/shard_map/ppermute | solution.py:880
  75.1 3.2 %collective-permute-done.9.refs_1_ = f32[360,128]{1,0:T(8,128)S(1)} collective-permute-done((f32[360,128]{1,0:T(8,128)S(1)}, f32[360,128]{1,0:T(8,128)S(1)}, u32[]{:S(2)}, u32[]{:S(2)}) %collective-permute-start.9) | collective-permute-done | bytes 184352 | tf_op jit(solution)/shard_map/ppermute | solution.py:880
  78.3 1.3 %collective-permute-done.10.refs_2_ = f32[360,128]{1,0:T(8,128)S(1)} collective-permute-done((f32[360,128]{1,0:T(8,128)S(1)}, f32[360,128]{1,0:T(8,128)S(1)}, u32[]{:S(2)}, u32[]{:S(2)}) %collective-permute-start.10) | collective-permute-done | bytes 184352 | tf_op jit(solution)/shard_map/ppermute | solution.py:880
  79.6 2.8 %collective-permute-done.11.refs_3_ = f32[360,128]{1,0:T(8,128)S(1)} collective-permute-done((f32[360,128]{1,0:T(8,128)S(1)}, f32[360,128]{1,0:T(8,128)S(1)}, u32[]{:S(2)}, u32[]{:S(2)}) %collective-permute-start.11) | collective-permute-done | bytes 184352 | tf_op jit(solution)/shard_map/ppermute | solution.py:880
  82.4 1.4 %collective-permute-done.15.refs_7_ = f32[360,128]{1,0:T(8,128)S(1)} collective-permute-done((f32[360,128]{1,0:T(8,128)S(1)}, f32[360,128]{1,0:T(8,128)S(1)}, u32[]{:S(2)}, u32[]{:S(2)}) %collective-permute-start.15) | collective-permute-done | bytes 184352 | tf_op jit(solution)/shard_map/ppermute | solution.py:880
  83.8 1.8 %finish.1 = (f32[1152,128]{1,0:T(8,128)}, f32[1,128]{1,0:T(1,128)}, f32[1,128]{1,0:T(1,128)}, f32[128,128]{1,0:T(8,128)}, f32[128,128]{1,0:T(8,128)}, /*index=5*...) custom-call(f32[360,128]{1,0:T(8,128)S(1)} %add_add_fusion.refs_0_, ...), custom_call_target="tpu_custom_call" | custom-call | tf_op jit(solution)/shard_map/finish/pallas_call | solution.py:977
  (38 shorter events, 0.2 us)
Async XLA Ops:
  31.8 1.5 %collective-permute-start.5 = (f32[360,128]{1,0:T(8,128)S(1)}, f32[360,128]{1,0:T(8,128)S(1)}, u32[]{:S(2)}, u32[]{:S(2)}) collective-permute-start(f32[360,128]{1,0:T(8,128)S(1)} %get-tuple-element.56), channel_id=1, source_target_pairs={{0,1},{1,0},{2,3},{3,2},{4,5},{5,4},{6,7},{7,6},{8,9},{9,8},{10,11... | collective-permute-start | bytes 552968 | tf_op jit(solution)/shard_map/ppermute | solution.py:880
  31.9 5.6 %collective-permute-start.3 = (f32[360,128]{1,0:T(8,128)S(1)}, f32[360,128]{1,0:T(8,128)S(1)}, u32[]{:S(2)}, u32[]{:S(2)}) collective-permute-start(f32[360,128]{1,0:T(8,128)S(1)} %get-tuple-element.54), channel_id=1, source_target_pairs={{0,1},{1,0},{2,3},{3,2},{4,5},{5,4},{6,7},{7,6},{8,9},{9,8},{10,11... | collective-permute-start | bytes 552968 | tf_op jit(solution)/shard_map/ppermute | solution.py:880
  32.4 7.8 %collective-permute-start.1 = (f32[360,128]{1,0:T(8,128)S(1)}, f32[360,128]{1,0:T(8,128)S(1)}, u32[]{:S(2)}, u32[]{:S(2)}) collective-permute-start(f32[360,128]{1,0:T(8,128)S(1)} %get-tuple-element.52), channel_id=1, source_target_pairs={{0,1},{1,0},{2,3},{3,2},{4,5},{5,4},{6,7},{7,6},{8,9},{9,8},{10,11... | collective-permute-start | bytes 552968 | tf_op jit(solution)/shard_map/ppermute | solution.py:880
  32.5 7.8 %collective-permute-start = (f32[360,128]{1,0:T(8,128)S(1)}, f32[360,128]{1,0:T(8,128)S(1)}, u32[]{:S(2)}, u32[]{:S(2)}) collective-permute-start(f32[360,128]{1,0:T(8,128)S(1)} %get-tuple-element.50), channel_id=1, source_target_pairs={{0,1},{1,0},{2,3},{3,2},{4,5},{5,4},{6,7},{7,6},{8,9},{9,8},{10,11... | collective-permute-start | bytes 552968 | tf_op jit(solution)/shard_map/ppermute | solution.py:880
  33.3 13.9 %collective-permute-start.6 = (f32[360,128]{1,0:T(8,128)S(1)}, f32[360,128]{1,0:T(8,128)S(1)}, u32[]{:S(2)}, u32[]{:S(2)}) collective-permute-start(f32[360,128]{1,0:T(8,128)S(1)} %add.52), channel_id=1, source_target_pairs={{0,4},{1,5},{2,6},{3,7},{4,0},{5,1},{6,2},{7,3},{8,12},{9,13},{10,... | collective-permute-start | bytes 552968 | tf_op jit(solution)/shard_map/ppermute | solution.py:880
  37.6 11.4 %collective-permute-start.4 = (f32[360,128]{1,0:T(8,128)S(1)}, f32[360,128]{1,0:T(8,128)S(1)}, u32[]{:S(2)}, u32[]{:S(2)}) collective-permute-start(f32[360,128]{1,0:T(8,128)S(1)} %add.50), channel_id=1, source_target_pairs={{0,2},{1,3},{2,0},{3,1},{4,6},{5,7},{6,4},{7,5},{8,10},{9,11},{10,... | collective-permute-start | bytes 552968 | tf_op jit(solution)/shard_map/ppermute | solution.py:880
  40.2 8.8 %collective-permute-start.2 = (f32[360,128]{1,0:T(8,128)S(1)}, f32[360,128]{1,0:T(8,128)S(1)}, u32[]{:S(2)}, u32[]{:S(2)}) collective-permute-start(f32[360,128]{1,0:T(8,128)S(1)} %add.48), channel_id=1, source_target_pairs={{0,6},{1,7},{2,4},{3,5},{4,2},{5,3},{6,0},{7,1},{8,14},{9,15},{10,... | collective-permute-start | bytes 552968 | tf_op jit(solution)/shard_map/ppermute | solution.py:880
  40.3 1.8 %copy-start.7 = (bf16[6,18,16,768]{3,2,1,0:T(8,128)(2,1)S(1)}, bf16[6,18,16,768]{3,2,1,0:T(8,128)(2,1)}, u32[]{:S(2)}) copy-start(bf16[6,18,16,768]{3,2,1,0:T(8,128)(2,1)} %get-tuple-element.57.grads) | copy-start | bytes 7962628
  42.1 1.1 %copy-start.11 = (bf16[256,1536]{1,0:T(8,128)(2,1)S(1)}, bf16[256,1536]{1,0:T(8,128)(2,1)}, u32[]{:S(2)}) copy-start(bf16[256,1536]{1,0:T(8,128)(2,1)} %get-tuple-element.58.weights) | copy-start | bytes 2359300
  43.2 20.6 %copy-start = (f32[3,3,128,128]{3,2,1,0:T(8,128)S(1)}, f32[3,3,128,128]{3,2,1,0:T(8,128)}, u32[]{:S(2)}) copy-start(f32[3,3,128,128]{3,2,1,0:T(8,128)} %param.24) | copy-start | bytes 1769476
  43.2 20.6 %copy-start.8 = (bf16[4,18,16,768]{3,2,1,0:T(8,128)(2,1)S(1)}, bf16[4,18,16,768]{3,2,1,0:T(8,128)(2,1)}, u32[]{:S(2)}) copy-start(bf16[4,18,16,768]{3,2,1,0:T(8,128)(2,1)} %get-tuple-element.46.inner_grads) | copy-start | bytes 5308420
  43.2 20.6 %copy-start.9 = (bf16[4,18,16,768]{3,2,1,0:T(8,128)(2,1)S(1)}, bf16[4,18,16,768]{3,2,1,0:T(8,128)(2,1)}, u32[]{:S(2)}) copy-start(bf16[4,18,16,768]{3,2,1,0:T(8,128)(2,1)} %get-tuple-element.48.grads) | copy-start | bytes 5308420
  43.2 20.6 %copy-start.10 = (bf16[256,1536]{1,0:T(8,128)(2,1)S(1)}, bf16[256,1536]{1,0:T(8,128)(2,1)}, u32[]{:S(2)}) copy-start(bf16[256,1536]{1,0:T(8,128)(2,1)} %get-tuple-element.47.inner_weights) | copy-start | bytes 2359300
  49.1 10.7 %collective-permute-start.7 = (f32[360,128]{1,0:T(8,128)S(1)}, f32[360,128]{1,0:T(8,128)S(1)}, u32[]{:S(2)}, u32[]{:S(2)}) collective-permute-start(f32[360,128]{1,0:T(8,128)S(1)} %add_add_fusion.1), channel_id=1, source_target_pairs={{0,8},{1,9},{2,10},{3,11},{4,12},{5,13},{6,14},{7,15},{8,0},{9,1},... | collective-permute-start | bytes 552968 | tf_op jit(solution)/shard_map/ppermute | solution.py:880
  59.8 11.7 %collective-permute-start.8 = (f32[360,128]{1,0:T(8,128)S(1)}, f32[360,128]{1,0:T(8,128)S(1)}, u32[]{:S(2)}, u32[]{:S(2)}) collective-permute-start(f32[360,128]{1,0:T(8,128)S(1)} %add.57), channel_id=1, source_target_pairs={{0,16},{1,17},{2,18},{3,19},{4,20},{5,21},{6,22},{7,23},{8,24},{9,... | collective-permute-start | bytes 552968 | tf_op jit(solution)/shard_map/ppermute | solution.py:880
  63.8 20.0 %copy-start.1 = (f32[128,128]{1,0:T(8,128)S(1)}, f32[128,128]{1,0:T(8,128)}, u32[]{:S(2)}) copy-start(f32[128,128]{1,0:T(8,128)} %refs_12_.3) | copy-start | bytes 196612
  63.8 20.0 %copy-start.2 = (f32[128,128]{1,0:T(8,128)S(1)}, f32[128,128]{1,0:T(8,128)}, u32[]{:S(2)}) copy-start(f32[128,128]{1,0:T(8,128)} %refs_11_.1) | copy-start | bytes 196612
  63.8 20.0 %copy-start.3 = (f32[128,128]{1,0:T(8,128)S(1)}, f32[128,128]{1,0:T(8,128)}, u32[]{:S(2)}) copy-start(f32[128,128]{1,0:T(8,128)} %refs_9_.1) | copy-start | bytes 196612
  63.9 20.0 %copy-start.4 = (f32[128,128]{1,0:T(8,128)S(1)}, f32[128,128]{1,0:T(8,128)}, u32[]{:S(2)}) copy-start(f32[128,128]{1,0:T(8,128)} %refs_8_.1) | copy-start | bytes 196612
  63.9 20.0 %copy-start.5 = (f32[9,9]{1,0:T(8,128)S(1)}, f32[9,9]{1,0:T(8,128)}, u32[]{:S(2)}) copy-start(f32[9,9]{1,0:T(8,128)} %refs_10_.1) | copy-start | bytes 976
  63.9 20.0 %copy-start.6 = (f32[9,9]{1,0:T(8,128)S(1)}, f32[9,9]{1,0:T(8,128)}, u32[]{:S(2)}) copy-start(f32[9,9]{1,0:T(8,128)} %refs_13_.3) | copy-start | bytes 976
  71.5 6.7 %collective-permute-start.9 = (f32[360,128]{1,0:T(8,128)S(1)}, f32[360,128]{1,0:T(8,128)S(1)}, u32[]{:S(2)}, u32[]{:S(2)}) collective-permute-start(f32[360,128]{1,0:T(8,128)S(1)} %add_add_fusion.refs_0_), channel_id=1, source_target_pairs={{0,2},{1,3},{2,0},{3,1},{4,6},{5,7},{6,4},{7,5},{8,10},{9,11},{10,... | collective-permute-start | bytes 552968 | tf_op jit(solution)/shard_map/ppermute | solution.py:880
  72.2 7.3 %collective-permute-start.10 = (f32[360,128]{1,0:T(8,128)S(1)}, f32[360,128]{1,0:T(8,128)S(1)}, u32[]{:S(2)}, u32[]{:S(2)}) collective-permute-start(f32[360,128]{1,0:T(8,128)S(1)} %add_add_fusion.refs_0_), channel_id=1, source_target_pairs={{0,4},{1,5},{2,6},{3,7},{4,0},{5,1},{6,2},{7,3},{8,12},{9,13},{10,... | collective-permute-start | bytes 552968 | tf_op jit(solution)/shard_map/ppermute | solution.py:880
  73.3 9.0 %collective-permute-start.11 = (f32[360,128]{1,0:T(8,128)S(1)}, f32[360,128]{1,0:T(8,128)S(1)}, u32[]{:S(2)}, u32[]{:S(2)}) collective-permute-start(f32[360,128]{1,0:T(8,128)S(1)} %add_add_fusion.refs_0_), channel_id=1, source_target_pairs={{0,6},{1,7},{2,4},{3,5},{4,2},{5,3},{6,0},{7,1},{8,14},{9,15},{10,... | collective-permute-start | bytes 552968 | tf_op jit(solution)/shard_map/ppermute | solution.py:880
  75.1 7.3 %collective-permute-start.12 = (f32[360,128]{1,0:T(8,128)S(1)}, f32[360,128]{1,0:T(8,128)S(1)}, u32[]{:S(2)}, u32[]{:S(2)}) collective-permute-start(f32[360,128]{1,0:T(8,128)S(1)} %add_add_fusion.refs_0_), channel_id=1, source_target_pairs={{0,1},{1,0},{2,3},{3,2},{4,5},{5,4},{6,7},{7,6},{8,9},{9,8},{10,11... | collective-permute-start | bytes 552968 | tf_op jit(solution)/shard_map/ppermute | solution.py:880
  78.3 4.1 %collective-permute-start.13 = (f32[360,128]{1,0:T(8,128)S(1)}, f32[360,128]{1,0:T(8,128)S(1)}, u32[]{:S(2)}, u32[]{:S(2)}) collective-permute-start(f32[360,128]{1,0:T(8,128)S(1)} %collective-permute-done.9.refs_1_), channel_id=1, source_target_pairs={{0,1},{1,0},{2,3},{3,2},{4,5},{5,4},{6,7},{7,6},{8,9},{9,8},{10,11... | collective-permute-start | bytes 552968 | tf_op jit(solution)/shard_map/ppermute | solution.py:880
  79.6 2.8 %collective-permute-start.14 = (f32[360,128]{1,0:T(8,128)S(1)}, f32[360,128]{1,0:T(8,128)S(1)}, u32[]{:S(2)}, u32[]{:S(2)}) collective-permute-start(f32[360,128]{1,0:T(8,128)S(1)} %collective-permute-done.10.refs_2_), channel_id=1, source_target_pairs={{0,1},{1,0},{2,3},{3,2},{4,5},{5,4},{6,7},{7,6},{8,9},{9,8},{10,11... | collective-permute-start | bytes 552968 | tf_op jit(solution)/shard_map/ppermute | solution.py:880
  82.4 1.4 %collective-permute-start.15 = (f32[360,128]{1,0:T(8,128)S(1)}, f32[360,128]{1,0:T(8,128)S(1)}, u32[]{:S(2)}, u32[]{:S(2)}) collective-permute-start(f32[360,128]{1,0:T(8,128)S(1)} %collective-permute-done.11.refs_3_), channel_id=1, source_target_pairs={{0,1},{1,0},{2,3},{3,2},{4,5},{5,4},{6,7},{7,6},{8,9},{9,8},{10,11... | collective-permute-start | bytes 552968 | tf_op jit(solution)/shard_map/ppermute | solution.py:880
where the time goes:
time: 84.5 us; the launch traced here: 85.8 us
  Pallas kernels  38.6 us (46%)
  starting transfers between devices  22.1 us (26%)
  waiting for transfers between devices  19.6 us (23%)
  local copies, waits for them, and re-layouts  2.94 us (3%)
  between operations  2.3 us (3%)
    pallas_call x1, Pallas kernels, run_task(): pl.pallas_call(partial(task_kernel, inputs + outputs + list(scratch)), ou...  29.9 us
    ppermute x16, starting transfers between devices, swap(): lax.ppermute(value, AXES, [(place, place ^ mask) for place in range(exten...  22.1 us
    ppermute x16, waiting for transfers between devices, swap(): lax.ppermute(value, AXES, [(place, place ^ mask) for place in range(exten...  19.6 us
    pallas_call x2, Pallas kernels, run_image_grads(): pl.pallas_call(kernel, out_shape=(jax.ShapeDtypeStruct(shape, BF16), pltp...  7.02 us
    unnamed x24, local copies, waits for them, and re-layouts  2.93 us
    pallas_call x1, Pallas kernels, run_finish(): pl.pallas_call(finish_kernel, out_shape=layer * 2, in_specs=[vmem] * 14,...  1.76 us
  transfers between devices with their start and end apart: 16, of which 8 were waited for; matrix products, arithmetic and copies ran while one was open for 0% of the time, Pallas kernels for 8%

commit v1 on v0

--- a/solution.py
+++ b/solution.py
@@ -496,8 +496,8 @@
 AT_OUTER, AT_INNER, AT_SMALL, AT_GAIN, HALF_ROWS = 9 * C, 10 * C, 11 * C, 11 * C + 16, 11 * C + 32
 QUARTER = HALF_ROWS // 4
 FETCHED = [
+    "support",
     "kernel_one",
-    "support",
     "gain_one",
     "shift_one",
     "gain_two",
@@ -706,15 +706,15 @@
     pools_q1, pools_q2 = (k.p1q, k.p2q), (k.p1q2, k.p2q2)
 
     cells_one, cells_two = ns_f * 1024.0, ns_f * 256.0
-    ready("kernel_one")
+    ready("support")
+    load_images(ns, k.support, k.xs)
+    ready("kernel_one", *NORMS)
     write_weights(k.w_a, tap_of(k.kernel_one))
-    ready("support", *NORMS)
     for name in FETCHED[6:]:
         fetches[name].start()
     gain_one, shift_one, gain_two, shift_two = (
         jnp.broadcast_to(getattr(k, name)[...], (8, C)) for name in NORMS
     )
-    load_images(ns, k.support, k.xs)
     conv_one(ns, [(k.xs, k.w_a)], keep(k.zs, alone))
     stats_one = statistics(ns, k.zs, cells_one, summed=k.sums[0], **one)
     activate(ns, k.zs, k.s1s, k.s2s, pools_one, stats_one, gain_one, shift_one, emit=pool_to(k.hs), **one)

time: 84.5 us -> 86.8 us (1.027); the launches traced: 85.8 us -> 86 us
  Pallas kernels: 38.6 us -> 32.8 us
  starting transfers between devices: 22.1 us -> 26.9 us
  waiting for transfers between devices: 19.6 us -> 20.9 us
    pallas_call x1, Pallas kernels: 29.9 us -> 25.1 us  [run_task(): pl.pallas_call(partial(task_kernel, inputs + outputs + list(scratch)), ou...]
    ppermute x16, starting transfers between devices: 22.1 us -> 26.9 us  [swap(): lax.ppermute(value, AXES, [(place, place ^ mask) for place in range(exten...]
    ppermute x16, waiting for transfers between devices: 19.6 us -> 20.9 us  [swap(): lax.ppermute(value, AXES, [(place, place ^ mask) for place in range(exten...]
    pallas_call x2, Pallas kernels: 7.02 us -> 6 us  [run_image_grads(): pl.pallas_call(kernel, out_shape=(jax.ShapeDtypeStruct(shape, BF16), pltp...]
  transfers between devices with their start and end apart: 16 -> 16, of which waited for: 8 -> 8; matrix products, arithmetic and copies ran while one was open for 0% -> 0% of each run, Pallas kernels for 8% -> 7%
where the time goes in v1:
time: 86.8 us; the launch traced here: 86 us
  Pallas kernels  32.8 us (38%)
  starting transfers between devices  26.9 us (31%)
  waiting for transfers between devices  20.9 us (24%)
  local copies, waits for them, and re-layouts  2.94 us (3%)
  between operations  2.27 us (3%)
    ppermute x16, starting transfers between devices, swap(): lax.ppermute(value, AXES, [(place, place ^ mask) for place in range(exten...  26.9 us
    pallas_call x1, Pallas kernels, run_task(): pl.pallas_call(partial(task_kernel, inputs + outputs + list(scratch)), ou...  25.1 us
    ppermute x16, waiting for transfers between devices, swap(): lax.ppermute(value, AXES, [(place, place ^ mask) for place in range(exten...  20.9 us
    pallas_call x2, Pallas kernels, run_image_grads(): pl.pallas_call(kernel, out_shape=(jax.ShapeDtypeStruct(shape, BF16), pltp...  6 us
    unnamed x24, local copies, waits for them, and re-layouts  2.94 us
    pallas_call x1, Pallas kernels, run_finish(): pl.pallas_call(finish_kernel, out_shape=layer * 2, in_specs=[vmem] * 14,...  1.76 us
  transfers between devices with their start and end apart: 16, of which 8 were waited for; matrix products, arithmetic and copies ran while one was open for 0% of the time, Pallas kernels for 7%

profile of v1, /device:TPU:0, one launch (start us, length us, event | category | flops | bytes accessed | tf_op | source)
XLA Modules:
  0.0 86.0 jit_solution(10270799377854840254)
XLA Ops:
  1.9 25.1 %task.1 = (bf16[6,8,8,128]{3,2,1,0:T(8,128)(2,1)}, bf16[6,18,16,768]{3,2,1,0:T(8,128)(2,1)}, bf16[256,1536]{1,0:T(8,128)(2,1)}, bf16[4,18,16,768]{3,2,1,0:T(8,12...) custom-call(s32[1]{0:T(128)S(6)} %copy.33.refs_0_.count, ...), custom_call_target="tpu_custom_call" | custom-call | tf_op jit(solution)/shard_map/task/pallas_call | solution.py:858
  27.0 0.1 collective-permute-start.5
  27.1 0.5 collective-permute-start.3
  27.6 0.1 collective-permute-start.1
  27.7 0.4 collective-permute-start
  28.1 0.4 collective-permute-done.5
  28.5 8.4 %collective-permute-start.6 = (f32[360,128]{1,0:T(8,128)S(1)}, f32[360,128]{1,0:T(8,128)S(1)}, u32[]{:S(2)}, u32[]{:S(2)}) collective-permute-start(f32[360,128]{1,0:T(8,128)S(1)} %add.52), channel_id=1, source_target_pairs={{0,4},{1,5},{2,6},{3,7},{4,0},{5,1},{6,2},{7,3},{8,12},{9,13},{10,... | collective-permute-start | bytes 552968 | tf_op jit(solution)/shard_map/ppermute | solution.py:880
  37.0 0.5 collective-permute-start.4
  37.5 1.4 %collective-permute-start.2 = (f32[360,128]{1,0:T(8,128)S(1)}, f32[360,128]{1,0:T(8,128)S(1)}, u32[]{:S(2)}, u32[]{:S(2)}) collective-permute-start(f32[360,128]{1,0:T(8,128)S(1)} %add.48), channel_id=1, source_target_pairs={{0,6},{1,7},{2,4},{3,5},{4,2},{5,3},{6,0},{7,1},{8,14},{9,15},{10,... | collective-permute-start | bytes 552968 | tf_op jit(solution)/shard_map/ppermute | solution.py:880
  38.8 1.7 %copy-done.7 = bf16[6,18,16,768]{3,2,1,0:T(8,128)(2,1)S(1)} copy-done((bf16[6,18,16,768]{3,2,1,0:T(8,128)(2,1)S(1)}, bf16[6,18,16,768]{3,2,1,0:T(8,128)(2,1)}, u32[]{:S(2)}) %copy-start.7) | copy-done | bytes 2654232
  40.6 1.1 %copy-done.11 = bf16[256,1536]{1,0:T(8,128)(2,1)S(1)} copy-done((bf16[256,1536]{1,0:T(8,128)(2,1)S(1)}, bf16[256,1536]{1,0:T(8,128)(2,1)}, u32[]{:S(2)}) %copy-start.11) | copy-done | bytes 786456
  41.7 3.0 %query_grad.1 = (bf16[6,32,32,128]{3,2,1,0:T(8,128)(2,1)}, f32[8,128]{1,0:T(8,128)S(1)}) custom-call(s32[1]{0:T(128)S(6)} %copy.34.refs_1_.count, bf16[6,18,16,768]{3,2,1,0:T(8,128)(2,1)S(1)} %copy-done.7, bf16[256,1536]{1,0:T(8,128)(2,1)S(1)} %copy-done.11, f32[8,128]{1,0:T(8,128)S(1)} %slice.16.after), custom_call_target="tpu_custom_call" | custom-call | flops 2415919104 | bytes 3145728 | tf_op jit(solution)/shard_map/query_grad/pallas_call | solution.py:476
  44.7 2.9 %collective-permute-done.4 = f32[360,128]{1,0:T(8,128)S(1)} collective-permute-done((f32[360,128]{1,0:T(8,128)S(1)}, f32[360,128]{1,0:T(8,128)S(1)}, u32[]{:S(2)}, u32[]{:S(2)}) %collective-permute-start.4) | collective-permute-done | bytes 184352 | tf_op jit(solution)/shard_map/ppermute | solution.py:880
  47.6 0.1 add_add_fusion.1
  47.7 1.7 %collective-permute-start.7 = (f32[360,128]{1,0:T(8,128)S(1)}, f32[360,128]{1,0:T(8,128)S(1)}, u32[]{:S(2)}, u32[]{:S(2)}) collective-permute-start(f32[360,128]{1,0:T(8,128)S(1)} %add_add_fusion.1), channel_id=1, source_target_pairs={{0,8},{1,9},{2,10},{3,11},{4,12},{5,13},{6,14},{7,15},{8,0},{9,1},... | collective-permute-start | bytes 552968 | tf_op jit(solution)/shard_map/ppermute | solution.py:880
  49.4 4.4 %collective-permute-done.7 = f32[360,128]{1,0:T(8,128)S(1)} collective-permute-done((f32[360,128]{1,0:T(8,128)S(1)}, f32[360,128]{1,0:T(8,128)S(1)}, u32[]{:S(2)}, u32[]{:S(2)}) %collective-permute-start.7) | collective-permute-done | bytes 184352 | tf_op jit(solution)/shard_map/ppermute | solution.py:880
  53.8 10.2 %collective-permute-start.8 = (f32[360,128]{1,0:T(8,128)S(1)}, f32[360,128]{1,0:T(8,128)S(1)}, u32[]{:S(2)}, u32[]{:S(2)}) collective-permute-start(f32[360,128]{1,0:T(8,128)S(1)} %add.57), channel_id=1, source_target_pairs={{0,16},{1,17},{2,18},{3,19},{4,20},{5,21},{6,22},{7,23},{8,24},{9,... | collective-permute-start | bytes 552968 | tf_op jit(solution)/shard_map/ppermute | solution.py:880
  64.0 0.0 copy-start.1
  64.0 0.0 copy-start.2
  64.0 0.0 copy-start.3
  64.1 0.0 copy-start.5
  64.1 0.0 copy-start.6
  64.1 3.0 %support_grad.1 = (bf16[4,32,32,128]{3,2,1,0:T(8,128)(2,1)}, f32[8,128]{1,0:T(8,128)S(1)}) custom-call(s32[1]{0:T(128)S(6)} %copy.33.refs_0_.count, bf16[4,18,16,768]{3,2,1,0:T(8,128)(2,1)S(1)} %copy-done.8, bf16[256,1536]{1,0:T(8,128)(2,1)S(1)} %copy-done.10, bf16[4,18,16,768]{3,2,1,0:T(8,128)(2,1)S(1)} %copy-done.9, f32[9,128,128]{2,1,0:T(8,128)S(1)} %bitcast.24, ...), custom_call_target="tpu_custom_call" | custom-call | flops 3221225472 | bytes 3145728 | tf_op jit(solution)/shard_map/support_grad/pallas_call | solution.py:476
  67.1 3.8 %collective-permute-done.8 = f32[360,128]{1,0:T(8,128)S(1)} collective-permute-done((f32[360,128]{1,0:T(8,128)S(1)}, f32[360,128]{1,0:T(8,128)S(1)}, u32[]{:S(2)}, u32[]{:S(2)}) %collective-permute-start.8) | collective-permute-done | bytes 184352 | tf_op jit(solution)/shard_map/ppermute | solution.py:880
  71.0 0.8 collective-permute-start.9
  71.8 1.6 %collective-permute-start.10 = (f32[360,128]{1,0:T(8,128)S(1)}, f32[360,128]{1,0:T(8,128)S(1)}, u32[]{:S(2)}, u32[]{:S(2)}) collective-permute-start(f32[360,128]{1,0:T(8,128)S(1)} %add_add_fusion.refs_0_), channel_id=1, source_target_pairs={{0,4},{1,5},{2,6},{3,7},{4,0},{5,1},{6,2},{7,3},{8,12},{9,13},{10,... | collective-permute-start | bytes 552968 | tf_op jit(solution)/shard_map/ppermute | solution.py:880
  73.4 1.2 %collective-permute-start.11 = (f32[360,128]{1,0:T(8,128)S(1)}, f32[360,128]{1,0:T(8,128)S(1)}, u32[]{:S(2)}, u32[]{:S(2)}) collective-permute-start(f32[360,128]{1,0:T(8,128)S(1)} %add_add_fusion.refs_0_), channel_id=1, source_target_pairs={{0,6},{1,7},{2,4},{3,5},{4,2},{5,3},{6,0},{7,1},{8,14},{9,15},{10,... | collective-permute-start | bytes 552968 | tf_op jit(solution)/shard_map/ppermute | solution.py:880
  74.6 3.2 %collective-permute-done.9.refs_1_ = f32[360,128]{1,0:T(8,128)S(1)} collective-permute-done((f32[360,128]{1,0:T(8,128)S(1)}, f32[360,128]{1,0:T(8,128)S(1)}, u32[]{:S(2)}, u32[]{:S(2)}) %collective-permute-start.9) | collective-permute-done | bytes 184352 | tf_op jit(solution)/shard_map/ppermute | solution.py:880
  77.7 1.6 %collective-permute-done.10.refs_2_ = f32[360,128]{1,0:T(8,128)S(1)} collective-permute-done((f32[360,128]{1,0:T(8,128)S(1)}, f32[360,128]{1,0:T(8,128)S(1)}, u32[]{:S(2)}, u32[]{:S(2)}) %collective-permute-start.10) | collective-permute-done | bytes 184352 | tf_op jit(solution)/shard_map/ppermute | solution.py:880
  79.3 3.2 %collective-permute-done.11.refs_3_ = f32[360,128]{1,0:T(8,128)S(1)} collective-permute-done((f32[360,128]{1,0:T(8,128)S(1)}, f32[360,128]{1,0:T(8,128)S(1)}, u32[]{:S(2)}, u32[]{:S(2)}) %collective-permute-start.11) | collective-permute-done | bytes 184352 | tf_op jit(solution)/shard_map/ppermute | solution.py:880
  82.6 1.4 %collective-permute-done.15.refs_7_ = f32[360,128]{1,0:T(8,128)S(1)} collective-permute-done((f32[360,128]{1,0:T(8,128)S(1)}, f32[360,128]{1,0:T(8,128)S(1)}, u32[]{:S(2)}, u32[]{:S(2)}) %collective-permute-start.15) | collective-permute-done | bytes 184352 | tf_op jit(solution)/shard_map/ppermute | solution.py:880
  84.1 1.8 %finish.1 = (f32[1152,128]{1,0:T(8,128)}, f32[1,128]{1,0:T(1,128)}, f32[1,128]{1,0:T(1,128)}, f32[128,128]{1,0:T(8,128)}, f32[128,128]{1,0:T(8,128)}, /*index=5*...) custom-call(f32[360,128]{1,0:T(8,128)S(1)} %add_add_fusion.refs_0_, ...), custom_call_target="tpu_custom_call" | custom-call | tf_op jit(solution)/shard_map/finish/pallas_call | solution.py:977
  (38 shorter events, 0.2 us)
Async XLA Ops:
  27.0 1.5 %collective-permute-start.5 = (f32[360,128]{1,0:T(8,128)S(1)}, f32[360,128]{1,0:T(8,128)S(1)}, u32[]{:S(2)}, u32[]{:S(2)}) collective-permute-start(f32[360,128]{1,0:T(8,128)S(1)} %get-tuple-element.56), channel_id=1, source_target_pairs={{0,1},{1,0},{2,3},{3,2},{4,5},{5,4},{6,7},{7,6},{8,9},{9,8},{10,11... | collective-permute-start | bytes 552968 | tf_op jit(solution)/shard_map/ppermute | solution.py:880
  27.1 9.8 %collective-permute-start.3 = (f32[360,128]{1,0:T(8,128)S(1)}, f32[360,128]{1,0:T(8,128)S(1)}, u32[]{:S(2)}, u32[]{:S(2)}) collective-permute-start(f32[360,128]{1,0:T(8,128)S(1)} %get-tuple-element.54), channel_id=1, source_target_pairs={{0,1},{1,0},{2,3},{3,2},{4,5},{5,4},{6,7},{7,6},{8,9},{9,8},{10,11... | collective-permute-start | bytes 552968 | tf_op jit(solution)/shard_map/ppermute | solution.py:880
  27.6 9.9 %collective-permute-start.1 = (f32[360,128]{1,0:T(8,128)S(1)}, f32[360,128]{1,0:T(8,128)S(1)}, u32[]{:S(2)}, u32[]{:S(2)}) collective-permute-start(f32[360,128]{1,0:T(8,128)S(1)} %get-tuple-element.52), channel_id=1, source_target_pairs={{0,1},{1,0},{2,3},{3,2},{4,5},{5,4},{6,7},{7,6},{8,9},{9,8},{10,11... | collective-permute-start | bytes 552968 | tf_op jit(solution)/shard_map/ppermute | solution.py:880
  27.7 11.2 %collective-permute-start = (f32[360,128]{1,0:T(8,128)S(1)}, f32[360,128]{1,0:T(8,128)S(1)}, u32[]{:S(2)}, u32[]{:S(2)}) collective-permute-start(f32[360,128]{1,0:T(8,128)S(1)} %get-tuple-element.50), channel_id=1, source_target_pairs={{0,1},{1,0},{2,3},{3,2},{4,5},{5,4},{6,7},{7,6},{8,9},{9,8},{10,11... | collective-permute-start | bytes 552968 | tf_op jit(solution)/shard_map/ppermute | solution.py:880
  28.5 16.2 %collective-permute-start.6 = (f32[360,128]{1,0:T(8,128)S(1)}, f32[360,128]{1,0:T(8,128)S(1)}, u32[]{:S(2)}, u32[]{:S(2)}) collective-permute-start(f32[360,128]{1,0:T(8,128)S(1)} %add.52), channel_id=1, source_target_pairs={{0,4},{1,5},{2,6},{3,7},{4,0},{5,1},{6,2},{7,3},{8,12},{9,13},{10,... | collective-permute-start | bytes 552968 | tf_op jit(solution)/shard_map/ppermute | solution.py:880
  37.0 10.6 %collective-permute-start.4 = (f32[360,128]{1,0:T(8,128)S(1)}, f32[360,128]{1,0:T(8,128)S(1)}, u32[]{:S(2)}, u32[]{:S(2)}) collective-permute-start(f32[360,128]{1,0:T(8,128)S(1)} %add.50), channel_id=1, source_target_pairs={{0,2},{1,3},{2,0},{3,1},{4,6},{5,7},{6,4},{7,5},{8,10},{9,11},{10,... | collective-permute-start | bytes 552968 | tf_op jit(solution)/shard_map/ppermute | solution.py:880
  37.5 10.1 %collective-permute-start.2 = (f32[360,128]{1,0:T(8,128)S(1)}, f32[360,128]{1,0:T(8,128)S(1)}, u32[]{:S(2)}, u32[]{:S(2)}) collective-permute-start(f32[360,128]{1,0:T(8,128)S(1)} %add.48), channel_id=1, source_target_pairs={{0,6},{1,7},{2,4},{3,5},{4,2},{5,3},{6,0},{7,1},{8,14},{9,15},{10,... | collective-permute-start | bytes 552968 | tf_op jit(solution)/shard_map/ppermute | solution.py:880
  38.8 1.8 %copy-start.7 = (bf16[6,18,16,768]{3,2,1,0:T(8,128)(2,1)S(1)}, bf16[6,18,16,768]{3,2,1,0:T(8,128)(2,1)}, u32[]{:S(2)}) copy-start(bf16[6,18,16,768]{3,2,1,0:T(8,128)(2,1)} %get-tuple-element.57.grads) | copy-start | bytes 7962628
  40.6 1.1 %copy-start.11 = (bf16[256,1536]{1,0:T(8,128)(2,1)S(1)}, bf16[256,1536]{1,0:T(8,128)(2,1)}, u32[]{:S(2)}) copy-start(bf16[256,1536]{1,0:T(8,128)(2,1)} %get-tuple-element.58.weights) | copy-start | bytes 2359300
  41.7 22.3 %copy-start = (f32[3,3,128,128]{3,2,1,0:T(8,128)S(1)}, f32[3,3,128,128]{3,2,1,0:T(8,128)}, u32[]{:S(2)}) copy-start(f32[3,3,128,128]{3,2,1,0:T(8,128)} %param.24) | copy-start | bytes 1769476
  41.7 22.3 %copy-start.8 = (bf16[4,18,16,768]{3,2,1,0:T(8,128)(2,1)S(1)}, bf16[4,18,16,768]{3,2,1,0:T(8,128)(2,1)}, u32[]{:S(2)}) copy-start(bf16[4,18,16,768]{3,2,1,0:T(8,128)(2,1)} %get-tuple-element.46.inner_grads) | copy-start | bytes 5308420
  41.7 22.3 %copy-start.9 = (bf16[4,18,16,768]{3,2,1,0:T(8,128)(2,1)S(1)}, bf16[4,18,16,768]{3,2,1,0:T(8,128)(2,1)}, u32[]{:S(2)}) copy-start(bf16[4,18,16,768]{3,2,1,0:T(8,128)(2,1)} %get-tuple-element.48.grads) | copy-start | bytes 5308420
  41.7 22.3 %copy-start.10 = (bf16[256,1536]{1,0:T(8,128)(2,1)S(1)}, bf16[256,1536]{1,0:T(8,128)(2,1)}, u32[]{:S(2)}) copy-start(bf16[256,1536]{1,0:T(8,128)(2,1)} %get-tuple-element.47.inner_weights) | copy-start | bytes 2359300
  47.7 6.1 %collective-permute-start.7 = (f32[360,128]{1,0:T(8,128)S(1)}, f32[360,128]{1,0:T(8,128)S(1)}, u32[]{:S(2)}, u32[]{:S(2)}) collective-permute-start(f32[360,128]{1,0:T(8,128)S(1)} %add_add_fusion.1), channel_id=1, source_target_pairs={{0,8},{1,9},{2,10},{3,11},{4,12},{5,13},{6,14},{7,15},{8,0},{9,1},... | collective-permute-start | bytes 552968 | tf_op jit(solution)/shard_map/ppermute | solution.py:880
  53.8 17.2 %collective-permute-start.8 = (f32[360,128]{1,0:T(8,128)S(1)}, f32[360,128]{1,0:T(8,128)S(1)}, u32[]{:S(2)}, u32[]{:S(2)}) collective-permute-start(f32[360,128]{1,0:T(8,128)S(1)} %add.57), channel_id=1, source_target_pairs={{0,16},{1,17},{2,18},{3,19},{4,20},{5,21},{6,22},{7,23},{8,24},{9,... | collective-permute-start | bytes 552968 | tf_op jit(solution)/shard_map/ppermute | solution.py:880
  64.0 20.0 %copy-start.1 = (f32[128,128]{1,0:T(8,128)S(1)}, f32[128,128]{1,0:T(8,128)}, u32[]{:S(2)}) copy-start(f32[128,128]{1,0:T(8,128)} %refs_12_.3) | copy-start | bytes 196612
  64.0 20.0 %copy-start.2 = (f32[128,128]{1,0:T(8,128)S(1)}, f32[128,128]{1,0:T(8,128)}, u32[]{:S(2)}) copy-start(f32[128,128]{1,0:T(8,128)} %refs_11_.1) | copy-start | bytes 196612
  64.0 20.0 %copy-start.3 = (f32[128,128]{1,0:T(8,128)S(1)}, f32[128,128]{1,0:T(8,128)}, u32[]{:S(2)}) copy-start(f32[128,128]{1,0:T(8,128)} %refs_9_.1) | copy-start | bytes 196612
  64.1 20.0 %copy-start.4 = (f32[128,128]{1,0:T(8,128)S(1)}, f32[128,128]{1,0:T(8,128)}, u32[]{:S(2)}) copy-start(f32[128,128]{1,0:T(8,128)} %refs_8_.1) | copy-start | bytes 196612
  64.1 20.0 %copy-start.5 = (f32[9,9]{1,0:T(8,128)S(1)}, f32[9,9]{1,0:T(8,128)}, u32[]{:S(2)}) copy-start(f32[9,9]{1,0:T(8,128)} %refs_10_.1) | copy-start | bytes 976
  64.1 20.0 %copy-start.6 = (f32[9,9]{1,0:T(8,128)S(1)}, f32[9,9]{1,0:T(8,128)}, u32[]{:S(2)}) copy-start(f32[9,9]{1,0:T(8,128)} %refs_13_.3) | copy-start | bytes 976
  71.0 6.7 %collective-permute-start.9 = (f32[360,128]{1,0:T(8,128)S(1)}, f32[360,128]{1,0:T(8,128)S(1)}, u32[]{:S(2)}, u32[]{:S(2)}) collective-permute-start(f32[360,128]{1,0:T(8,128)S(1)} %add_add_fusion.refs_0_), channel_id=1, source_target_pairs={{0,2},{1,3},{2,0},{3,1},{4,6},{5,7},{6,4},{7,5},{8,10},{9,11},{10,... | collective-permute-start | bytes 552968 | tf_op jit(solution)/shard_map/ppermute | solution.py:880
  71.8 7.5 %collective-permute-start.10 = (f32[360,128]{1,0:T(8,128)S(1)}, f32[360,128]{1,0:T(8,128)S(1)}, u32[]{:S(2)}, u32[]{:S(2)}) collective-permute-start(f32[360,128]{1,0:T(8,128)S(1)} %add_add_fusion.refs_0_), channel_id=1, source_target_pairs={{0,4},{1,5},{2,6},{3,7},{4,0},{5,1},{6,2},{7,3},{8,12},{9,13},{10,... | collective-permute-start | bytes 552968 | tf_op jit(solution)/shard_map/ppermute | solution.py:880
  73.4 9.2 %collective-permute-start.11 = (f32[360,128]{1,0:T(8,128)S(1)}, f32[360,128]{1,0:T(8,128)S(1)}, u32[]{:S(2)}, u32[]{:S(2)}) collective-permute-start(f32[360,128]{1,0:T(8,128)S(1)} %add_add_fusion.refs_0_), channel_id=1, source_target_pairs={{0,6},{1,7},{2,4},{3,5},{4,2},{5,3},{6,0},{7,1},{8,14},{9,15},{10,... | collective-permute-start | bytes 552968 | tf_op jit(solution)/shard_map/ppermute | solution.py:880
  74.6 8.0 %collective-permute-start.12 = (f32[360,128]{1,0:T(8,128)S(1)}, f32[360,128]{1,0:T(8,128)S(1)}, u32[]{:S(2)}, u32[]{:S(2)}) collective-permute-start(f32[360,128]{1,0:T(8,128)S(1)} %add_add_fusion.refs_0_), channel_id=1, source_target_pairs={{0,1},{1,0},{2,3},{3,2},{4,5},{5,4},{6,7},{7,6},{8,9},{9,8},{10,11... | collective-permute-start | bytes 552968 | tf_op jit(solution)/shard_map/ppermute | solution.py:880
  77.7 4.9 %collective-permute-start.13 = (f32[360,128]{1,0:T(8,128)S(1)}, f32[360,128]{1,0:T(8,128)S(1)}, u32[]{:S(2)}, u32[]{:S(2)}) collective-permute-start(f32[360,128]{1,0:T(8,128)S(1)} %collective-permute-done.9.refs_1_), channel_id=1, source_target_pairs={{0,1},{1,0},{2,3},{3,2},{4,5},{5,4},{6,7},{7,6},{8,9},{9,8},{10,11... | collective-permute-start | bytes 552968 | tf_op jit(solution)/shard_map/ppermute | solution.py:880
  79.3 3.3 %collective-permute-start.14 = (f32[360,128]{1,0:T(8,128)S(1)}, f32[360,128]{1,0:T(8,128)S(1)}, u32[]{:S(2)}, u32[]{:S(2)}) collective-permute-start(f32[360,128]{1,0:T(8,128)S(1)} %collective-permute-done.10.refs_2_), channel_id=1, source_target_pairs={{0,1},{1,0},{2,3},{3,2},{4,5},{5,4},{6,7},{7,6},{8,9},{9,8},{10,11... | collective-permute-start | bytes 552968 | tf_op jit(solution)/shard_map/ppermute | solution.py:880
  82.6 1.4 %collective-permute-start.15 = (f32[360,128]{1,0:T(8,128)S(1)}, f32[360,128]{1,0:T(8,128)S(1)}, u32[]{:S(2)}, u32[]{:S(2)}) collective-permute-start(f32[360,128]{1,0:T(8,128)S(1)} %collective-permute-done.11.refs_3_), channel_id=1, source_target_pairs={{0,1},{1,0},{2,3},{3,2},{4,5},{5,4},{6,7},{7,6},{8,9},{9,8},{10,11... | collective-permute-start | bytes 552968 | tf_op jit(solution)/shard_map/ppermute | solution.py:880
